TPU v7x, 128 devices: a whole 4x4x4 slice. The times are simulated.
128 devices in a mesh: dp: 8 (over z, y_lo), ctx: 16 (over y_hi, x, core).
Axes of the slice: x: 4, y: 4 (y_hi: 2, y_lo: 2; y = y_hi * 2 + y_lo), z: 4, core: 2. Of those that a mesh axis runs over, the one named last changes fastest.
Arguments:
- queries: bfloat16 [8, 2048, 8192], P('dp', 'ctx'), may hold values from -6 to 6
- keys: bfloat16 [8, 2048, 8192], P('dp', 'ctx'), may hold values from -6 to 6
- values: bfloat16 [8, 2048, 8192], P('dp', 'ctx'), may hold values from -6 to 6
- out_grad: bfloat16 [8, 2048, 8192], P('dp', 'ctx'), may hold values from -6 to 6
- residue: float32 [16, 8192], P(None, 'ctx'), may hold values from -0.12 to 0.12
- rate: float32 [16, 8192], P(None, 'ctx'), may hold values from 0.00024414062 to 0.05
Outputs:
- query_grad: bfloat16 [8, 2048, 8192], P('dp', 'ctx')
- key_grad: bfloat16 [8, 2048, 8192], P('dp', 'ctx')
- value_grad: bfloat16 [8, 2048, 8192], P('dp', 'ctx')
- residue_grad: float32 [16, 8192], P(None, 'ctx')
- rate_grad: float32 [16, 8192], P(None, 'ctx')
All inputs are finite; a program needn't handle non-finite values.
Results may differ from a plain program's by a relative error of at most 0.017.
Values may be sent and summed in bfloat16 or wider, within the bound.
No kernel may reach another device: no remote copies, remote signals or barrier semaphores. Data moves between devices by JAX's collectives and lax.ppermute only.
A program may use at most 128 MiB of HBM per device.

v0:
```python
import math

import jax
import jax.numpy as jnp
from jax import lax
from jax.sharding import PartitionSpec as P


def angle_table(row_count, col_count, period):
    product = (
        jnp.arange(row_count, dtype=jnp.int32)[:, None]
        * jnp.arange(col_count, dtype=jnp.int32)[None, :]
        % period
    )
    phase_angle = product.astype(jnp.float32) * (2.0 * math.pi / period)
    return (jnp.cos(phase_angle), -jnp.sin(phase_angle))


def make_tables(full_len):
    outer = full_len // 64
    first_cos, first_sin = angle_table(outer, outer // 2, outer)
    twist_cos, twist_sin = angle_table(outer, 64, full_len)
    inner_cos, inner_sin = angle_table(64, 64, 64)
    return (
        first_cos.astype(jnp.bfloat16),
        first_sin.astype(jnp.bfloat16),
        twist_cos,
        twist_sin,
        inner_cos.astype(jnp.bfloat16),
        inner_sin.astype(jnp.bfloat16),
    )


def narrow_einsum(form, left, right):
    return jnp.einsum(form, left, right, preferred_element_type=jnp.float32)


def forward_dft(signal, tables):
    first_cos, first_sin, twist_cos, twist_sin, inner_cos, inner_sin = tables
    part_real = narrow_einsum("ka,atc->ktc", first_cos, signal)
    part_imag = narrow_einsum("ka,atc->ktc", first_sin, signal)
    turn_cos = twist_cos[:, :, None]
    turn_sin = twist_sin[:, :, None]
    turned_real = (part_real * turn_cos - part_imag * turn_sin).astype(jnp.bfloat16)
    turned_imag = (part_real * turn_sin + part_imag * turn_cos).astype(jnp.bfloat16)
    out_real = narrow_einsum("ktc,tj->kjc", turned_real, inner_cos) - narrow_einsum(
        "ktc,tj->kjc", turned_imag, inner_sin
    )
    out_imag = narrow_einsum("ktc,tj->kjc", turned_real, inner_sin) + narrow_einsum(
        "ktc,tj->kjc", turned_imag, inner_cos
    )
    return (out_real, out_imag)


def inverse_dft(spec_real, spec_imag, tables, full_len):
    first_cos, first_sin, twist_cos, twist_sin, inner_cos, inner_sin = tables
    spec_real = spec_real.astype(jnp.bfloat16)
    spec_imag = spec_imag.astype(jnp.bfloat16)
    back_real = narrow_einsum("kjc,tj->ktc", spec_real, inner_cos) + narrow_einsum(
        "kjc,tj->ktc", spec_imag, inner_sin
    )
    back_imag = narrow_einsum("kjc,tj->ktc", spec_imag, inner_cos) - narrow_einsum(
        "kjc,tj->ktc", spec_real, inner_sin
    )
    turn_cos = twist_cos[:, :, None]
    turn_sin = twist_sin[:, :, None]
    turned_real = (back_real * turn_cos + back_imag * turn_sin).astype(jnp.bfloat16)
    turned_imag = (back_imag * turn_cos - back_real * turn_sin).astype(jnp.bfloat16)
    signal = narrow_einsum("ka,ktc->atc", first_cos, turned_real) + narrow_einsum(
        "ka,ktc->atc", first_sin, turned_imag
    )
    return signal / full_len


def channel_work(gated, mixed, residue, rate):
    seq_len = gated.shape[1]
    chans = gated.shape[2]
    full_len = 2 * seq_len
    half_rows = seq_len // 64
    tables = make_tables(full_len)
    chan_block = min(256, chans)
    block_count = chans // chan_block
    gated_grid = gated.reshape(half_rows, 64, chans)
    mixed_grid = mixed.reshape(half_rows, 64, chans)
    lags = (
        jnp.arange(half_rows, dtype=jnp.int32)[:, None] * 64
        + jnp.arange(64, dtype=jnp.int32)[None, :]
    ).astype(jnp.float32)
    mode_count = residue.shape[0]

    def block_step(number, carry):
        conv_all, back_all, res_all, rate_all = carry
        start = number * chan_block
        gate_part = lax.dynamic_slice_in_dim(gated_grid, start, chan_block, 2)
        mix_part = lax.dynamic_slice_in_dim(mixed_grid, start, chan_block, 2)
        res_part = lax.dynamic_slice_in_dim(residue, start, chan_block, 1)
        rate_part = lax.dynamic_slice_in_dim(rate, start, chan_block, 1)
        decays = jnp.exp(-rate_part[:, None, None, :] * lags[None, :, :, None])
        filt = jnp.sum(res_part[:, None, None, :] * decays, 0).astype(jnp.bfloat16)
        filt_real, filt_imag = forward_dft(filt, tables)
        mix_real, mix_imag = forward_dft(mix_part, tables)
        gate_real, gate_imag = forward_dft(gate_part, tables)
        conv = inverse_dft(
            filt_real * mix_real - filt_imag * mix_imag,
            filt_real * mix_imag + filt_imag * mix_real,
            tables,
            full_len,
        )
        back = inverse_dft(
            filt_real * gate_real + filt_imag * gate_imag,
            filt_real * gate_imag - filt_imag * gate_real,
            tables,
            full_len,
        )
        lagged = inverse_dft(
            mix_real * gate_real + mix_imag * gate_imag,
            mix_real * gate_imag - mix_imag * gate_real,
            tables,
            full_len,
        )
        res_grad = jnp.sum(lagged[None] * decays, (1, 2))
        rate_grad = -res_part * jnp.sum(lags[None, :, :, None] * lagged[None] * decays, (1, 2))
        conv_all = lax.dynamic_update_slice_in_dim(conv_all, conv.astype(jnp.bfloat16), start, 2)
        back_all = lax.dynamic_update_slice_in_dim(back_all, back.astype(jnp.bfloat16), start, 2)
        res_all = lax.dynamic_update_slice_in_dim(res_all, res_grad, start, 1)
        rate_all = lax.dynamic_update_slice_in_dim(rate_all, rate_grad, start, 1)
        return (conv_all, back_all, res_all, rate_all)

    initial = (
        jnp.zeros((half_rows, 64, chans), jnp.bfloat16),
        jnp.zeros((half_rows, 64, chans), jnp.bfloat16),
        jnp.zeros((mode_count, chans), jnp.float32),
        jnp.zeros((mode_count, chans), jnp.float32),
    )
    conv_all, back_all, res_all, rate_all = lax.fori_loop(0, block_count, block_step, initial)
    return (
        conv_all.reshape(1, seq_len, chans),
        back_all.reshape(1, seq_len, chans),
        res_all,
        rate_all,
    )


def times_bf16(left, right):
    return (left.astype(jnp.float32) * right.astype(jnp.float32)).astype(jnp.bfloat16)


def body(queries, keys, values, out_grad, residue, rate):
    gated = times_bf16(out_grad, queries)
    mixed = times_bf16(keys, values)
    gated_chan, mixed_chan = (
        lax.all_to_all(gated, "ctx", split_axis=2, concat_axis=1, tiled=True),
        lax.all_to_all(mixed, "ctx", split_axis=2, concat_axis=1, tiled=True),
    )
    conv, back, res_local, rate_local = channel_work(gated_chan, mixed_chan, residue, rate)
    conv_seq, back_seq = (
        lax.all_to_all(conv, "ctx", split_axis=1, concat_axis=2, tiled=True),
        lax.all_to_all(back, "ctx", split_axis=1, concat_axis=2, tiled=True),
    )
    query_grad = times_bf16(out_grad, conv_seq)
    key_grad = times_bf16(back_seq, values)
    value_grad = times_bf16(back_seq, keys)
    residue_grad, rate_grad = (
        lax.psum(res_local.astype(jnp.bfloat16), "dp").astype(jnp.float32),
        lax.psum(rate_local.astype(jnp.bfloat16), "dp").astype(jnp.float32),
    )
    return (query_grad, key_grad, value_grad, residue_grad, rate_grad)


def solution(mesh):
    return jax.shard_map(
        body,
        mesh=mesh,
        in_specs=(
            P("dp", "ctx", None),
            P("dp", "ctx", None),
            P("dp", "ctx", None),
            P("dp", "ctx", None),
            P(None, "ctx"),
            P(None, "ctx"),
        ),
        out_specs=(
            P("dp", "ctx", None),
            P("dp", "ctx", None),
            P("dp", "ctx", None),
            P(None, "ctx"),
            P(None, "ctx"),
        ),
        check_vma=False,
    )
```

profile of v0, /device:TPU:1, one launch (start us, length us, event | category | flops | bytes accessed | tf_op | source)
XLA Modules:
  0.0 640.1 jit_solution(5561025010407229622)
XLA Ops:
  0.6 3.2 copy.229
  3.9 4.5 copy.230
  10.5 33.3 %copy.356 = bf16[1,128,8192]{1,0,2:T(2,128)(2,1)} copy(bf16[1,128,8192]{1,2,0:T(8,128)(2,1)S(1)} %fusion.305) | data formatting | bytes 4194304 | tf_op jit(solution)/shard_map/convert_element_type | solution.py:145
  44.4 45.2 %reduce = bf16[8192,128]{1,0:T(8,128)(2,1)S(1)} reduce(bf16[8192,1,128]{2,1,0:T(2,128)(2,1)} %bitcast.324, bf16[]{:T(256)} %broadcast.170), dimensions={1}, to_apply=%bitcast.203.reduce_sub_computation | reduce | bytes 4194306
  91.6 8.8 %all-to-all-start = ((bf16[16,2,32768]{2,1,0:T(2,128)(2,1)}), bf16[16,2,32768]{2,1,0:T(2,128)(2,1)}, u32[]{:S(2)}, u32[]{:S(2)}) async-start(bf16[16,2,32768]{2,1,0:T(2,128)(2,1)} %reshape.95), calls=%async_computation | async-start | bytes 4194304 | tf_op jit(solution)/shard_map/all_to_all | solution.py:153
  103.6 4.5 copy.233
  110.2 33.3 %copy.355 = bf16[1,128,8192]{1,0,2:T(2,128)(2,1)} copy(bf16[1,128,8192]{1,2,0:T(8,128)(2,1)S(1)} %fusion.302) | data formatting | bytes 4194304 | tf_op jit(solution)/shard_map/convert_element_type | solution.py:145
  143.5 45.2 %reduce.1 = bf16[8192,128]{1,0:T(8,128)(2,1)S(1)} reduce(bf16[8192,1,128]{2,1,0:T(2,128)(2,1)} %bitcast.326, bf16[]{:T(256)} %broadcast.170), dimensions={1}, to_apply=%bitcast.202.reduce_sub_computation | reduce | bytes 4194306
  190.7 7.2 %all-to-all-start.1 = ((bf16[16,2,32768]{2,1,0:T(2,128)(2,1)}), bf16[16,2,32768]{2,1,0:T(2,128)(2,1)}, u32[]{:S(2)}, u32[]{:S(2)}) async-start(bf16[16,2,32768]{2,1,0:T(2,128)(2,1)} %reshape.97), calls=%async_computation.1 | async-start | bytes 4194304 | tf_op jit(solution)/shard_map/all_to_all | solution.py:152
  198.0 10.4 %reshape.96 = bf16[8192,1,128]{2,1,0:T(2,128)(2,1)} reshape(bf16[16,2,32768]{2,1,0:T(2,128)(2,1)} %all-to-all-done) | data formatting | bytes 4194304
  208.4 3.8 copy.279
  215.1 11.6 %all-to-all-done.1 = bf16[16,2,32768]{2,1,0:T(2,128)(2,1)} async-done(((bf16[16,2,32768]{2,1,0:T(2,128)(2,1)}), bf16[16,2,32768]{2,1,0:T(2,128)(2,1)}, u32[]{:S(2)}, u32[]{:S(2)}) %all-to-all-start.1) | async-done | bytes 2097184 | tf_op jit(solution)/shard_map/all_to_all | solution.py:152
  226.7 10.4 %reshape.98 = bf16[8192,1,128]{2,1,0:T(2,128)(2,1)} reshape(bf16[16,2,32768]{2,1,0:T(2,128)(2,1)} %all-to-all-done.1) | data formatting | bytes 4194304
  237.1 3.8 copy.280
  240.9 3.9 copy.235
  247.9 212.2 %while.21 = (s32[]{:T(128)}, bf16[32,64,512]{2,1,0:T(8,128)(2,1)}, bf16[32,64,512]{2,1,0:T(8,128)(2,1)}, bf16[16,512]{1,0:T(8,128)(2,1)S(1)}, bf16[16,512]{1,0:T...) while((s32[]{:T(128)}, bf16[32,64,512]{2,1,0:T(8,128)(2,1)}, ...), condition=%wide.region_4.5_spmd.clone.clone, body=%wide.region_0.4_spmd.clone.clone.sunk | while | flops 4179564544 | bytes 475472704 | solution.py:135
  253.1 5.8 fusion.491
  286.9 11.8 %multiply_reduce_fusion.4 = (f32[16,256]{1,0:T(8,128)S(1)}, bf16[16,256]{1,0:T(8,128)(2,1)S(1)}, bf16[32,64,256]{2,1,0:T(8,128)(2,1)S(1)}) fusion(f32[32,64,256]{2,1,0:T(8,128)S(1)} %copy.414, f32[32,64]{1,0:T(8,128)S(1)} %copy.415, f32[16,256]{1,0:T(8,128)S(1)} %dynamic-slice_negate_fusion.2, f32[32,64,256]{2,1,0:T(8,128)S(1)} %copy.416, ...), kind=kLoop, calls=%fused_computation.7.clone.1 | loop fusion | flops 58187776 | bytes 5308416 | tf_op jit(solution)/shard_map/while/body/eval_jaxpr/reduce_sum | solution.py:122
  299.7 4.1 fusion.502
  303.8 3.8 fusion.504
  309.4 3.8 convolution_add_fusion.12
  313.2 9.7 %fusion.505 = (bf16[64,64,256]{2,1,0:T(8,128)(2,1)}, bf16[64,64,256]{2,1,0:T(8,128)(2,1)}, bf16[64,64,256]{2,1,0:T(8,128)(2,1)}, bf16[64,64,256]{2,1,0:T(8,128)(2,1)}) fusion(f32[64,256,64]{1,2,0:T(8,128)} %convolution_add_fusion.12, f32[64,256,64]{1,2,0:T(8,128)S(1)} %convolution_subtract_fusion.11, f32[64,256,64]{1,2,0:T(8,128)S(1)} %convolution_add_fusion.11, ...), kind=kOutput, calls=%fused_computation.64.clone.1 | convolution fusion | flops 152109056 | bytes 35651584 | tf_op jit(solution)/shard_map/while/body/eval_jaxpr/ktc,tj->kjc/dot_general | solution.py:35
  332.7 4.8 fusion.510
  337.5 3.4 fusion.511
  355.0 5.6 fusion.491
  388.8 11.8 %multiply_reduce_fusion.4 = (f32[16,256]{1,0:T(8,128)S(1)}, bf16[16,256]{1,0:T(8,128)(2,1)S(1)}, bf16[32,64,256]{2,1,0:T(8,128)(2,1)S(1)}) fusion(f32[32,64,256]{2,1,0:T(8,128)S(1)} %copy.414, f32[32,64]{1,0:T(8,128)S(1)} %copy.415, f32[16,256]{1,0:T(8,128)S(1)} %dynamic-slice_negate_fusion.2, f32[32,64,256]{2,1,0:T(8,128)S(1)} %copy.416, ...), kind=kLoop, calls=%fused_computation.7.clone.1 | loop fusion | flops 58187776 | bytes 5308416 | tf_op jit(solution)/shard_map/while/body/eval_jaxpr/reduce_sum | solution.py:122
  401.6 4.1 fusion.502
  405.7 3.8 fusion.504
  411.3 3.8 convolution_add_fusion.12
  415.1 9.6 %fusion.505 = (bf16[64,64,256]{2,1,0:T(8,128)(2,1)}, bf16[64,64,256]{2,1,0:T(8,128)(2,1)}, bf16[64,64,256]{2,1,0:T(8,128)(2,1)}, bf16[64,64,256]{2,1,0:T(8,128)(2,1)}) fusion(f32[64,256,64]{1,2,0:T(8,128)} %convolution_add_fusion.12, f32[64,256,64]{1,2,0:T(8,128)S(1)} %convolution_subtract_fusion.11, f32[64,256,64]{1,2,0:T(8,128)S(1)} %convolution_add_fusion.11, ...), kind=kOutput, calls=%fused_computation.64.clone.1 | convolution fusion | flops 152109056 | bytes 35651584 | tf_op jit(solution)/shard_map/while/body/eval_jaxpr/ktc,tj->kjc/dot_general | solution.py:35
  434.5 4.6 fusion.510
  439.2 3.4 fusion.511
  460.2 7.5 %copy.354 = bf16[1,2048,512]{2,0,1:T(2,128)(2,1)} copy(bf16[1,2048,512]{2,1,0:T(8,128)(2,1)} %bitcast.335) | data formatting | bytes 4194304 | tf_op jit(solution)/shard_map/reshape | solution.py:137
  467.6 14.1 %reduce.2 = bf16[2048,512]{1,0:T(8,128)(2,1)S(1)} reduce(bf16[2048,1,512]{2,1,0:T(2,128)(2,1)} %bitcast.329, bf16[]{:T(256)} %broadcast.170), dimensions={1}, to_apply=%bitcast.201.reduce_sub_computation | reduce | bytes 4194306
  484.5 5.5 all-to-all-start.2
  490.0 42.9 %all-reduce = (bf16[16,512]{1,0:T(8,128)(2,1)S(1)}, bf16[16,512]{1,0:T(8,128)(2,1)S(1)}) all-reduce(bf16[16,512]{1,0:T(8,128)(2,1)S(1)} %get-tuple-element.434, bf16[16,512]{1,0:T(8,128)(2,1)S(1)} %get-tuple-element.435), channel_id=1, replica_groups=mesh['dp'=8,'ctx'=16] {'dp'}, use_global_device_ids=true, to_apply=%region_5.6 | all-reduce | flops 16384 | bytes 65536 | tf_op jit(solution)/shard_map/psum | solution.py:164
  534.1 7.4 %copy.353 = bf16[1,2048,512]{2,0,1:T(2,128)(2,1)} copy(bf16[1,2048,512]{2,1,0:T(8,128)(2,1)} %bitcast.334) | data formatting | bytes 4194304 | tf_op jit(solution)/shard_map/reshape | solution.py:138
  541.6 15.4 %reduce.3 = bf16[2048,512]{1,0:T(8,128)(2,1)} reduce(bf16[2048,1,512]{2,1,0:T(2,128)(2,1)} %bitcast.325, bf16[]{:T(256)} %broadcast.170), dimensions={1}, to_apply=%bitcast.200.reduce_sub_computation | reduce | bytes 4194306
  557.0 4.5 reshape.101
  561.5 15.6 %all-to-all-start.3 = ((bf16[16,2,32768]{2,1,0:T(2,128)(2,1)}), bf16[16,2,32768]{2,1,0:T(2,128)(2,1)}, u32[]{:S(2)}, u32[]{:S(2)}) async-start(bf16[16,2,32768]{2,1,0:T(2,128)(2,1)} %reshape.101), calls=%async_computation.3 | async-start | bytes 4194304 | tf_op jit(solution)/shard_map/all_to_all | solution.py:158
  577.1 6.8 %reshape.100 = bf16[2048,1,512]{2,1,0:T(2,128)(2,1)} reshape(bf16[16,2,32768]{2,1,0:T(2,128)(2,1)S(1)} %all-to-all-done.2) | data formatting | bytes 4194304
  589.2 5.5 copy.241
  594.7 3.9 fusion.303
  598.6 4.1 copy.246
  605.8 10.4 %reshape.102 = bf16[2048,1,512]{2,1,0:T(2,128)(2,1)} reshape(bf16[16,2,32768]{2,1,0:T(2,128)(2,1)} %all-to-all-done.3) | data formatting | bytes 4194304
  621.6 5.5 copy.245
  627.1 5.7 fusion.304
  632.8 4.2 copy.248
  (177 shorter events, 147.4 us)
Async XLA Ops:
  3.9 4.5 copy-start.8
  91.6 99.1 %all-to-all-start = ((bf16[16,2,32768]{2,1,0:T(2,128)(2,1)}), bf16[16,2,32768]{2,1,0:T(2,128)(2,1)}, u32[]{:S(2)}, u32[]{:S(2)}) async-start(bf16[16,2,32768]{2,1,0:T(2,128)(2,1)} %reshape.95), calls=%async_computation | async-start | bytes 4194304 | tf_op jit(solution)/shard_map/all_to_all | solution.py:153
  103.6 4.5 copy-start.10
  190.7 35.9 %all-to-all-start.1 = ((bf16[16,2,32768]{2,1,0:T(2,128)(2,1)}), bf16[16,2,32768]{2,1,0:T(2,128)(2,1)}, u32[]{:S(2)}, u32[]{:S(2)}) async-start(bf16[16,2,32768]{2,1,0:T(2,128)(2,1)} %reshape.97), calls=%async_computation.1 | async-start | bytes 4194304 | tf_op jit(solution)/shard_map/all_to_all | solution.py:152
  244.8 3.1 copy-start.17
  244.8 3.1 copy-start.18
  248.1 2.1 copy-start.6
  303.8 5.6 copy-start.3
  322.9 2.5 copy-start.2
  326.3 1.6 copy-start.1
  327.9 1.6 copy-start.4
  329.5 1.6 copy-start
  337.5 3.4 copy-start.5
  344.3 1.7 copy-start.12
  344.3 2.2 copy-start.14
  346.5 3.4 copy-start.7
  347.9 1.3 copy-start.13
  347.9 2.0 copy-start.15
  350.1 2.1 copy-start.6
  405.7 5.6 copy-start.3
  424.8 2.6 copy-start.2
  428.2 1.6 copy-start.1
  429.7 1.6 copy-start.4
  431.3 1.6 copy-start
  439.2 3.4 copy-start.5
  445.9 1.7 copy-start.12
  445.9 2.2 copy-start.14
  448.1 3.4 copy-start.7
  449.6 1.3 copy-start.13
  449.6 2.0 copy-start.15
  484.5 77.0 %all-to-all-start.2 = ((bf16[16,2,32768]{2,1,0:T(2,128)(2,1)}), bf16[16,2,32768]{2,1,0:T(2,128)(2,1)S(1)}, u32[]{:S(2)}, u32[]{:S(2)}) async-start(bf16[16,2,32768]{2,1,0:T(2,128)(2,1)} %reshape.99), calls=%async_computation.2 | async-start | bytes 4194304 | tf_op jit(solution)/shard_map/all_to_all | solution.py:157
  561.5 44.3 %all-to-all-start.3 = ((bf16[16,2,32768]{2,1,0:T(2,128)(2,1)}), bf16[16,2,32768]{2,1,0:T(2,128)(2,1)}, u32[]{:S(2)}, u32[]{:S(2)}) async-start(bf16[16,2,32768]{2,1,0:T(2,128)(2,1)} %reshape.101), calls=%async_computation.3 | async-start | bytes 4194304 | tf_op jit(solution)/shard_map/all_to_all | solution.py:158
  589.2 5.5 copy-start.11
  621.6 5.5 copy-start.9
  632.8 4.2 copy-start.16
where the time goes:
time: 651 us; the launch traced here: 640 us
  local copies, waits for them, and re-layouts  213 us (33%)
  other arithmetic  169 us (26%)
  matrix products  153 us (24%)
  blocking collectives  42.9 us (7%)
  starting transfers between devices  37.1 us (6%)
  waiting for transfers between devices  14.8 us (2%)
  loops' own time  9.56 us (1%)
    dot_general x72, matrix products, narrow_einsum(): return jnp.einsum(form, left, right, preferred_element_type=jnp.float32)  153 us
    unnamed x4, other arithmetic  120 us
    unnamed x32, local copies, waits for them, and re-layouts  84.1 us
    convert_element_type x2, local copies, waits for them, and re-layouts, times_bf16(): (left.astype(jnp.float32) * right.astype(jnp.float32)).astype(jnp.bfloat16)  66.5 us
    psum x1, blocking collectives, body(): lax.psum(res_local.astype(jnp.bfloat16), 'dp').astype(jnp.float32)  42.9 us
    reduce_sum x2, other arithmetic, block_step(): jnp.sum(lags[None, :, :, None] * lagged[None] * decays, (1, 2))  23.6 us
    all_to_all x1, starting transfers between devices, body(): lax.all_to_all(back, 'ctx', split_axis=1, concat_axis=2, tiled=True)  15.6 us
    convert_element_type x4, other arithmetic, times_bf16(): (left.astype(jnp.float32) * right.astype(jnp.float32)).astype(jnp.bfloat16)  13.9 us
  transfers between devices with their start and end apart: 4, of which 2 were waited for; matrix products, arithmetic and copies ran while one was open for 25% of the time, Pallas kernels for 0%

commit v1 on v0

v1 whole, which is shorter than its diff:
```python
import jax
import jax.numpy as jnp
from jax import lax
from jax.experimental import pallas as pl
from jax.experimental.pallas import tpu as pltpu
from jax.sharding import PartitionSpec as P

LEN = 128
MODES = 16
GROUP = 1024
F32 = jnp.float32
BF16 = jnp.bfloat16


def params(vmem=32):
    return pltpu.CompilerParams(vmem_limit_bytes=vmem * 1024 * 1024)


def cost(ops, moved):
    return pl.CostEstimate(flops=ops, bytes_accessed=moved, transcendentals=0)


def product(left, right):
    return (left.astype(F32) * right.astype(F32)).astype(BF16)


def gate_kernel(keys, values, out_grad, queries, x_out, g_out):
    for j in range(8):
        lanes = pl.ds(128 * j, 128)
        rows = pl.ds(j, LEN, stride=8)
        x_out[rows, :] = product(keys[:, lanes], values[:, lanes]).astype(F32)
        g_out[rows, :] = product(out_grad[:, lanes], queries[:, lanes]).astype(F32)


def spread(block, scratch, base=0):
    for m in range(MODES):
        for h in range(2):
            scratch[pl.ds(8 * m + 4 * h, 4), :] = block[h, pl.ds(base + 4 * m, 4), :]


def decays(rate, scratch):
    spread(rate, scratch)
    scratch[...] = jnp.exp(-scratch[...])


def modes_of(scratch, first=0, count=MODES):
    return tuple(scratch[pl.ds(8 * m, 8), :] for m in range(first, first + count))


def gather_rows(out, base, mode, state):
    for h in range(2):
        out[h, pl.ds(base + 4 * mode, 4), :] = state[4 * h : 4 * h + 4]


def row(t):
    return pl.ds(pl.multiple_of(8 * t, 8), 8)


def state_kernel(rate, x, g, out, lam_s):
    decays(rate, lam_s)
    lam = modes_of(lam_s)
    zero = jnp.zeros((8, 128), F32)

    def step(t, carry):
        fwd, bwd = carry
        xt = x[row(t), :]
        gt = g[row(LEN - 1 - t), :]
        fwd = tuple(l * s + xt for l, s in zip(lam, fwd))
        bwd = tuple(l * s + gt for l, s in zip(lam, bwd))
        return fwd, bwd

    fwd, bwd = lax.fori_loop(0, LEN, step, ((zero,) * MODES, (zero,) * MODES), unroll=2)
    for m in range(MODES):
        gather_rows(out, 0, m, fwd[m])
        gather_rows(out, 64, m, bwd[m])


def grad_kernel(rate, x, g, out, lam_s, wide):
    decays(rate, lam_s)
    zero = jnp.zeros((8, 128), F32)
    part = 8
    for first in range(0, MODES, part):
        lam = modes_of(lam_s, first, part)

        def step(t, carry):
            h, p, hg, pg = carry
            xt = x[row(t), :]
            gt = g[row(t), :]
            q = tuple(l * s for l, s in zip(lam, h))
            h = tuple(s + xt for s in q)
            p = tuple(l * s + u for l, s, u in zip(lam, p, q))
            hg = tuple(s + gt * u for s, u in zip(hg, h))
            pg = tuple(s + gt * u for s, u in zip(pg, p))
            return h, p, hg, pg

        h, p, hg, pg = lax.fori_loop(0, LEN, step, ((zero,) * part,) * 4, unroll=2)
        for m in range(part):
            gather_rows(wide, 0, first + m, p[m])
            gather_rows(wide, 128, first + m, hg[m])
            gather_rows(wide, 192, first + m, pg[m])
    lam = modes_of(lam_s)

    def back_step(t, carry):
        a, b = carry
        gt = g[row(LEN - 1 - t), :]
        q = tuple(l * s for l, s in zip(lam, a))
        a = tuple(s + gt for s in q)
        b = tuple(l * s + u for l, s, u in zip(lam, b, q))
        return a, b

    a, b = lax.fori_loop(0, LEN, back_step, ((zero,) * MODES,) * 2, unroll=2)
    for m in range(MODES):
        gather_rows(wide, 64, m, b[m])
    out[...] = wide[...].astype(BF16)


def total(terms):
    terms = list(terms)
    while len(terms) > 1:
        terms = [u + v for u, v in zip(terms[::2], terms[1::2])]
    return terms[0]


def local_kernel(rate, residue, x, g, conv, back, lam_s, res_s):
    decays(rate, lam_s)
    spread(residue, res_s)
    lam = modes_of(lam_s)
    res = modes_of(res_s)
    zero = jnp.zeros((8, 128), F32)

    def run(source, target, place):
        def step(t, h):
            at = row(place(t))
            xt = source[at, :]
            h = tuple(l * s + xt for l, s in zip(lam, h))
            target[at, :] = total(r * s for r, s in zip(res, h))
            return h

        lax.fori_loop(0, LEN, step, (zero,) * MODES, unroll=2)

    run(x, conv, lambda t: t)
    run(g, back, lambda t: LEN - 1 - t)


def scan_kernel(sums, rate, residue, out):
    lam = jnp.exp(-rate[...])
    far = jnp.exp(-float(LEN) * rate[...])
    scale = residue[...] * lam
    count = sums.shape[0]
    state = jnp.zeros((64, 128), F32)
    for d in range(count):
        out[d, 0:64, :] = scale * state
        state = far * state + sums[d, 0:64, :]
    state = jnp.zeros((64, 128), F32)
    for d in range(count - 1, -1, -1):
        out[d, 64:128, :] = scale * state
        state = far * state + sums[d, 64:128, :]


def owner_grad_kernel(sums, parts, rate, residue, out):
    lam = jnp.exp(-rate[...])
    far = jnp.exp(-float(LEN) * rate[...])
    zero = jnp.zeros((64, 128), F32)
    h, q, hg, pg, hb, qb = zero, zero, zero, zero, zero, zero
    for d in range(sums.shape[0]):
        b = sums[d, 64:128, :]
        hg = hg + parts[d, 128:192, :].astype(F32)
        pg = pg + parts[d, 192:256, :].astype(F32)
        hb = hb + h * b
        qb = qb + h * (parts[d, 64:128, :].astype(F32) + b) + q * b
        q = far * (q + float(LEN) * h) + parts[d, 0:64, :].astype(F32)
        h = far * h + sums[d, 0:64, :]
    out[0:64, :] = hg + lam * hb
    out[64:128, :] = -residue[...] * (pg + lam * qb)


def finish_kernel(rate, ends, conv, back, out_grad, keys, values, query_out, key_out, value_out, lam_s, head_s, tail_s, conv_s, back_s):
    decays(rate, lam_s)
    spread(ends, head_s)
    spread(ends, tail_s, 64)
    lam = modes_of(lam_s)

    def step(t, carry):
        head, tail = carry
        up, down = row(t), row(LEN - 1 - t)
        conv_s[up, :] = conv[up, :] + total(head)
        back_s[down, :] = back[down, :] + total(tail)
        return tuple(l * s for l, s in zip(lam, head)), tuple(l * s for l, s in zip(lam, tail))

    lax.fori_loop(0, LEN, step, (modes_of(head_s), modes_of(tail_s)), unroll=2)
    for j in range(8):
        lanes = pl.ds(128 * j, 128)
        rows = pl.ds(j, LEN, stride=8)
        c = conv_s[rows, :].astype(BF16)
        b = back_s[rows, :].astype(BF16)
        query_out[:, lanes] = product(out_grad[:, lanes], c)
        key_out[:, lanes] = product(b, values[:, lanes])
        value_out[:, lanes] = product(b, keys[:, lanes])


def wide_spec():
    return pl.BlockSpec((LEN, GROUP), lambda p: (0, p))


def tall_spec():
    return pl.BlockSpec((GROUP, 128), lambda p: (p, 0))


def owner_spec(rows):
    return pl.BlockSpec((2, rows, 128), lambda p: (p, 0, 0))


def registers(count):
    return pltpu.VMEM((8 * count, 128), F32)


def exchange(array):
    return lax.all_to_all(array, "ctx", split_axis=0, concat_axis=0, tiled=True)


def body(queries, keys, values, out_grad, residue, rate):
    owners = 16
    chans = queries.shape[2]
    groups = chans // GROUP
    flat = [a.reshape(LEN, chans) for a in (keys, values, out_grad, queries)]
    tall = jax.ShapeDtypeStruct((groups * GROUP, 128), F32)
    work = LEN * chans * MODES
    rate_own = rate.reshape(64, 128)
    residue_own = residue.reshape(64, 128)
    rate_all = exchange(jnp.broadcast_to(rate_own[None], (owners, 64, 128)))
    x, g = pl.pallas_call(
        gate_kernel,
        grid=(groups,),
        in_specs=[wide_spec()] * 4,
        out_specs=[tall_spec()] * 2,
        out_shape=[tall, tall],
        compiler_params=params(),
        cost_estimate=cost(LEN * chans * 4, LEN * chans * 16),
        name="gate",
    )(*flat)
    sums = pl.pallas_call(
        state_kernel,
        grid=(groups,),
        in_specs=[owner_spec(64), tall_spec(), tall_spec()],
        out_specs=owner_spec(128),
        out_shape=jax.ShapeDtypeStruct((owners, 128, 128), F32),
        scratch_shapes=[registers(MODES)],
        compiler_params=params(),
        cost_estimate=cost(4 * work, LEN * chans * 8),
        name="states",
    )(rate_all, x, g)
    sums_own = exchange(sums)
    residue_all = exchange(jnp.broadcast_to(residue_own[None], (owners, 64, 128)))
    parts = pl.pallas_call(
        grad_kernel,
        grid=(groups,),
        in_specs=[owner_spec(64), tall_spec(), tall_spec()],
        out_specs=owner_spec(256),
        out_shape=jax.ShapeDtypeStruct((owners, 256, 128), BF16),
        scratch_shapes=[registers(MODES), pltpu.VMEM((2, 256, 128), F32)],
        compiler_params=params(),
        cost_estimate=cost(12 * work, LEN * chans * 8),
        name="local_grads",
    )(rate_all, x, g)
    ends_own = pl.pallas_call(
        scan_kernel,
        out_shape=jax.ShapeDtypeStruct((owners, 128, 128), F32),
        compiler_params=params(),
        name="scan",
    )(sums_own, rate_own, residue_own)
    ends = exchange(ends_own)
    parts_own = exchange(parts)
    conv, back = pl.pallas_call(
        local_kernel,
        grid=(groups,),
        in_specs=[owner_spec(64), owner_spec(64), tall_spec(), tall_spec()],
        out_specs=[tall_spec()] * 2,
        out_shape=[tall, tall],
        scratch_shapes=[registers(MODES)] * 2,
        compiler_params=params(),
        cost_estimate=cost(8 * work, LEN * chans * 16),
        name="local_conv",
    )(rate_all, residue_all, x, g)
    grads = pl.pallas_call(
        owner_grad_kernel,
        out_shape=jax.ShapeDtypeStruct((128, 128), F32),
        compiler_params=params(),
        name="owner_grads",
    )(sums_own, parts_own, rate_own, residue_own)
    for bit in (1, 2, 4):
        grads = grads + lax.ppermute(grads, "dp", [(i, i ^ bit) for i in range(8)])
    flat_out = jax.ShapeDtypeStruct((LEN, chans), BF16)
    query_grad, key_grad, value_grad = pl.pallas_call(
        finish_kernel,
        grid=(groups,),
        in_specs=[owner_spec(64), owner_spec(128), tall_spec(), tall_spec()] + [wide_spec()] * 3,
        out_specs=[wide_spec()] * 3,
        out_shape=[flat_out] * 3,
        scratch_shapes=[registers(MODES)] * 3 + [pltpu.VMEM((GROUP, 128), F32)] * 2,
        compiler_params=params(),
        cost_estimate=cost(4 * work, LEN * chans * 20),
        name="finish",
    )(rate_all, ends, conv, back, flat[2], flat[0], flat[1])
    shape = queries.shape
    return (
        query_grad.reshape(shape),
        key_grad.reshape(shape),
        value_grad.reshape(shape),
        grads[:64].reshape(residue.shape),
        grads[64:].reshape(rate.shape),
    )


def solution(mesh):
    wide = P("dp", "ctx", None)
    narrow = P(None, "ctx")
    return jax.shard_map(
        body,
        mesh=mesh,
        in_specs=(wide,) * 4 + (narrow,) * 2,
        out_specs=(wide,) * 3 + (narrow,) * 2,
        check_vma=False,
    )
```

time: 651 us -> 214 us (0.33); the launches traced: 640 us -> 211 us
  local copies, waits for them, and re-layouts: 213 us -> 33.6 us
  other arithmetic: 169 us -> 0.03 us
  matrix products: 153 us -> 0 us
  Pallas kernels: 0 us -> 98 us
  blocking collectives: 42.9 us -> 0 us
  waiting for transfers between devices: 14.8 us -> 41.2 us
  loops' own time: 9.56 us -> 0 us
    dot_general x72 -> x0, matrix products: 153 us -> none  [narrow_einsum(): return jnp.einsum(form, left, right, preferred_element_type=jnp.float32)]
    unnamed x4 -> x0, other arithmetic: 120 us -> none
    pallas_call x0 -> x7, Pallas kernels: none -> 98 us  [the longest x1 39.7 us: body(): pl.pallas_call(grad_kernel, grid=(groups,), in_specs=[owner_spec(64), tal...]
    convert_element_type x6 -> x0, local copies, waits for them, and re-layouts: 77.7 us -> none  [the longest x2 66.5 us: times_bf16(): (left.astype(jnp.float32) * right.astype(jnp.float32)).astype(jnp.bfloat16)]
    unnamed x32 -> x34, local copies, waits for them, and re-layouts: 84.1 us -> 29 us
    psum x1 -> x0, blocking collectives: 42.9 us -> none  [body(): lax.psum(res_local.astype(jnp.bfloat16), 'dp').astype(jnp.float32)]
    convert_element_type x12 -> x0, other arithmetic: 25.1 us -> none  [the longest x4 13.9 us: times_bf16(): (left.astype(jnp.float32) * right.astype(jnp.float32)).astype(jnp.bfloat16)]
    reduce_sum x2 -> x0, other arithmetic: 23.6 us -> none  [block_step(): jnp.sum(lags[None, :, :, None] * lagged[None] * decays, (1, 2))]
  transfers between devices with their start and end apart: 4 -> 8, of which waited for: 2 -> 4; matrix products, arithmetic and copies ran while one was open for 25% -> 1% of each run, Pallas kernels for 0% -> 38%
where the time goes in v1:
time: 214 us; the launch traced here: 211 us
  Pallas kernels  98 us (46%)
  waiting for transfers between devices  41.2 us (19%)
  starting transfers between devices  37.9 us (18%)
  local copies, waits for them, and re-layouts  33.6 us (16%)
    pallas_call x1, Pallas kernels, body(): pl.pallas_call(grad_kernel, grid=(groups,), in_specs=[owner_spec(64), tal...  39.7 us
    all_to_all x5, starting transfers between devices, exchange(): return lax.all_to_all(array, 'ctx', split_axis=0, concat_axis=0, tiled=True)  32.2 us
    unnamed x34, local copies, waits for them, and re-layouts  29 us
    all_to_all x5, waiting for transfers between devices, exchange(): return lax.all_to_all(array, 'ctx', split_axis=0, concat_axis=0, tiled=True)  26.9 us
    pallas_call x1, Pallas kernels, body(): pl.pallas_call(local_kernel, grid=(groups,), in_specs=[owner_spec(64), ow...  21.2 us
    pallas_call x1, Pallas kernels, body(): pl.pallas_call(finish_kernel, grid=(groups,), in_specs=[owner_spec(64), o...  18.3 us
    pallas_call x1, Pallas kernels, body(): pl.pallas_call(state_kernel, grid=(groups,), in_specs=[owner_spec(64), ta...  14.3 us
    ppermute x3, waiting for transfers between devices, body(): grads = grads + lax.ppermute(grads, 'dp', [(i, i ^ bit) for i in range(8)])  14.3 us
  transfers between devices with their start and end apart: 8, of which 4 were waited for; matrix products, arithmetic and copies ran while one was open for 1% of the time, Pallas kernels for 38%

profile of v1, /device:TPU:1, one launch (start us, length us, event | category | flops | bytes accessed | tf_op | source)
XLA Modules:
  0.0 211.5 jit_solution(4000783652501454006)
XLA Ops:
  0.6 0.0 copy-start.6
  0.6 0.9 broadcast_in_dim.12.rate
  1.6 0.8 broadcast_in_dim.13
  2.4 8.4 %all-to-all-start = ((f32[16,64,128]{2,1,0:T(8,128)}), f32[16,64,128]{2,1,0:T(8,128)S(1)}, u32[]{:S(2)}, u32[]{:S(2)}) async-start(f32[16,64,128]{2,1,0:T(8,128)} %broadcast_in_dim.13), calls=%async_computation | async-start | bytes 1048576 | tf_op jit(solution)/shard_map/all_to_all | solution.py:218
  10.8 0.8 reshape.47.residue
  11.6 10.6 %all-to-all-done.rate = f32[16,64,128]{2,1,0:T(8,128)S(1)} async-done(((f32[16,64,128]{2,1,0:T(8,128)}), f32[16,64,128]{2,1,0:T(8,128)S(1)}, u32[]{:S(2)}, u32[]{:S(2)}) %all-to-all-start) | async-done | bytes 524320 | tf_op jit(solution)/shard_map/all_to_all | solution.py:218
  22.2 0.8 broadcast_in_dim.14
  23.1 4.4 %all-to-all-start.3 = ((f32[16,64,128]{2,1,0:T(8,128)}), f32[16,64,128]{2,1,0:T(8,128)S(1)}, u32[]{:S(2)}, u32[]{:S(2)}) async-start(f32[16,64,128]{2,1,0:T(8,128)} %broadcast_in_dim.14), calls=%async_computation.3 | async-start | bytes 1048576 | tf_op jit(solution)/shard_map/all_to_all | solution.py:218
  27.5 0.0 copy-done.6
  27.5 0.0 copy-start.8
  27.5 1.6 copy-done.8
  29.1 1.6 copy-done.10
  30.7 1.6 copy-done.16
  32.3 3.0 %gate.1 = (f32[8192,128]{1,0:T(8,128)S(1)}, f32[8192,128]{1,0:T(8,128)S(1)}) custom-call(bf16[128,8192]{1,0:T(8,128)(2,1)S(1)} %bitcast.7, bf16[128,8192]{1,0:T(8,128)(2,1)S(1)} %bitcast.9, bf16[128,8192]{1,0:T(8,128)(2,1)S(1)} %bitcast.11, bf16[128,8192]{1,0:T(8,128)(2,1)S(1)} %bitcast.13), custom_call_target="tpu_custom_call" | custom-call | flops 4194304 | bytes 16777216 | tf_op jit(solution)/shard_map/gate/pallas_call | solution.py:231
  35.3 14.3 %states.1 = f32[16,128,128]{2,1,0:T(8,128)} custom-call(f32[16,64,128]{2,1,0:T(8,128)S(1)} %all-to-all-done.rate, f32[8192,128]{1,0:T(8,128)S(1)} %get-tuple-element.12.x, f32[8192,128]{1,0:T(8,128)S(1)} %get-tuple-element.13.g), custom_call_target="tpu_custom_call" | custom-call | flops 67108864 | bytes 8388608 | tf_op jit(solution)/shard_map/states/pallas_call | solution.py:241
  49.6 2.0 copy-done
  51.5 2.0 copy-done.3
  53.6 0.0 all-to-all-done.3.residue
  53.6 7.3 %all-to-all-start.1 = ((f32[16,128,128]{2,1,0:T(8,128)}), f32[16,128,128]{2,1,0:T(8,128)S(1)}, u32[]{:S(2)}, u32[]{:S(2)}) async-start(f32[16,128,128]{2,1,0:T(8,128)} %states.1), calls=%async_computation.1 | async-start | bytes 2097152 | tf_op jit(solution)/shard_map/all_to_all | solution.py:218
  60.9 2.2 %copy-done.1 = f32[8192,128]{1,0:T(8,128)S(1)} copy-done((f32[8192,128]{1,0:T(8,128)S(1)}, f32[8192,128]{1,0:T(8,128)}, u32[]{:S(2)}) %copy-start.1) | copy-done | bytes 4194328
  63.1 2.2 %copy-done.4 = f32[8192,128]{1,0:T(8,128)S(1)} copy-done((f32[8192,128]{1,0:T(8,128)S(1)}, f32[8192,128]{1,0:T(8,128)}, u32[]{:S(2)}) %copy-start.4) | copy-done | bytes 4194328
  65.2 39.7 %local_grads.1 = bf16[16,256,128]{2,1,0:T(8,128)(2,1)} custom-call(f32[16,64,128]{2,1,0:T(8,128)S(1)} %all-to-all-done.rate, f32[8192,128]{1,0:T(8,128)S(1)} %copy-done.1, f32[8192,128]{1,0:T(8,128)S(1)} %copy-done.4), custom_call_target="tpu_custom_call" | custom-call | flops 201326592 | bytes 8388608 | tf_op jit(solution)/shard_map/local_grads/pallas_call | solution.py:254
  105.0 0.0 all-to-all-done.1.sums
  105.0 7.2 %all-to-all-start.4 = ((bf16[16,256,128]{2,1,0:T(8,128)(2,1)}), bf16[16,256,128]{2,1,0:T(8,128)(2,1)S(1)}, u32[]{:S(2)}, u32[]{:S(2)}) async-start(bf16[16,256,128]{2,1,0:T(8,128)(2,1)} %local_grads.1), calls=%async_computation.4 | async-start | bytes 2097152 | tf_op jit(solution)/shard_map/all_to_all | solution.py:218
  112.2 1.1 scan.1
  113.3 16.3 %all-to-all-done.4.parts = bf16[16,256,128]{2,1,0:T(8,128)(2,1)S(1)} async-done(((bf16[16,256,128]{2,1,0:T(8,128)(2,1)}), bf16[16,256,128]{2,1,0:T(8,128)(2,1)S(1)}, u32[]{:S(2)}, u32[]{:S(2)}) %all-to-all-start.4) | async-done | bytes 1048608 | tf_op jit(solution)/shard_map/all_to_all | solution.py:218
  129.6 4.8 %all-to-all-start.2 = ((f32[16,128,128]{2,1,0:T(8,128)}), f32[16,128,128]{2,1,0:T(8,128)}, u32[]{:S(2)}, u32[]{:S(2)}) async-start(f32[16,128,128]{2,1,0:T(8,128)} %scan.1), calls=%async_computation.2 | async-start | bytes 2097152 | tf_op jit(solution)/shard_map/all_to_all | solution.py:218
  134.4 0.3 owner_grads.1
  134.7 0.5 collective-permute-start
  135.2 12.2 %collective-permute-done = f32[128,128]{1,0:T(8,128)S(1)} collective-permute-done((f32[128,128]{1,0:T(8,128)S(1)}, f32[128,128]{1,0:T(8,128)S(1)}, u32[]{:S(2)}, u32[]{:S(2)}) %collective-permute-start) | collective-permute-done | bytes 65568 | tf_op jit(solution)/shard_map/ppermute | solution.py:291
  147.4 1.7 collective-permute-start.1
  149.2 2.1 collective-permute-done.1
  151.2 3.5 %collective-permute-start.2 = (f32[128,128]{1,0:T(8,128)S(1)}, f32[128,128]{1,0:T(8,128)S(1)}, u32[]{:S(2)}, u32[]{:S(2)}) collective-permute-start(f32[128,128]{1,0:T(8,128)S(1)} %add.10), channel_id=1, source_target_pairs={{0,64},{16,80},{32,96},{48,112},{64,0},{80,16},{96,32},{112,48},{1... | collective-permute-start | bytes 196616 | tf_op jit(solution)/shard_map/ppermute | solution.py:291
  154.7 2.2 %copy-done.2 = f32[8192,128]{1,0:T(8,128)S(1)} copy-done((f32[8192,128]{1,0:T(8,128)S(1)}, f32[8192,128]{1,0:T(8,128)}, u32[]{:S(2)}) %copy-start.2) | copy-done | bytes 4194328
  156.9 2.2 %copy-done.5 = f32[8192,128]{1,0:T(8,128)S(1)} copy-done((f32[8192,128]{1,0:T(8,128)S(1)}, f32[8192,128]{1,0:T(8,128)}, u32[]{:S(2)}) %copy-start.5) | copy-done | bytes 4194328
  159.1 21.2 %local_conv.1 = (f32[8192,128]{1,0:T(8,128)S(1)}, f32[8192,128]{1,0:T(8,128)S(1)}) custom-call(f32[16,64,128]{2,1,0:T(8,128)S(1)} %all-to-all-done.rate, f32[16,64,128]{2,1,0:T(8,128)S(1)} %all-to-all-done.3.residue, f32[8192,128]{1,0:T(8,128)S(1)} %copy-done.2, f32[8192,128]{1,0:T(8,128)S(1)} %copy-done.5), custom_call_target="tpu_custom_call" | custom-call | flops 134217728 | bytes 16777216 | tf_op jit(solution)/shard_map/local_conv/pallas_call | solution.py:273
  180.4 0.0 copy-start.12
  180.4 1.9 copy-done.12
  182.3 2.0 copy-done.14
  184.3 0.0 collective-permute-done.2
  184.4 0.6 reshape.51
  185.0 0.6 reshape.52
  185.6 0.0 all-to-all-done.2.ends
  185.6 1.6 copy-done.9
  187.2 1.6 copy-done.11
  188.8 2.2 %copy-done.13 = f32[8192,128]{1,0:T(8,128)S(1)} copy-done((f32[8192,128]{1,0:T(8,128)S(1)}, f32[8192,128]{1,0:T(8,128)}, u32[]{:S(2)}) %copy-start.13) | copy-done | bytes 4194328
  191.0 2.2 %copy-done.15 = f32[8192,128]{1,0:T(8,128)S(1)} copy-done((f32[8192,128]{1,0:T(8,128)S(1)}, f32[8192,128]{1,0:T(8,128)}, u32[]{:S(2)}) %copy-start.15) | copy-done | bytes 4194328
  193.2 18.3 %finish.1 = (bf16[128,8192]{1,0:T(8,128)(2,1)}, bf16[128,8192]{1,0:T(8,128)(2,1)}, bf16[128,8192]{1,0:T(8,128)(2,1)}) custom-call(f32[16,64,128]{2,1,0:T(8,128)S(1)} %all-to-all-done.rate, f32[16,128,128]{2,1,0:T(8,128)} %all-to-all-done.2.ends, f32[8192,128]{1,0:T(8,128)S(1)} %copy-done.13, f32[8192,128]{1,0:T(8,128)S(1)} %copy-done.15, ...), custom_call_target="tpu_custom_call" | custom-call | flops 67108864 | bytes 20971520 | tf_op jit(solution)/shard_map/finish/pallas_call | solution.py:293
  (19 shorter events, 0.1 us)
Async XLA Ops:
  0.6 26.9 %copy-start.6 = (bf16[1,128,8192]{2,1,0:T(8,128)(2,1)S(1)}, bf16[1,128,8192]{2,1,0:T(8,128)(2,1)}, u32[]{:S(2)}) copy-start(bf16[1,128,8192]{2,1,0:T(8,128)(2,1)} %param.7) | copy-start | bytes 6291460
  2.4 19.8 %all-to-all-start = ((f32[16,64,128]{2,1,0:T(8,128)}), f32[16,64,128]{2,1,0:T(8,128)S(1)}, u32[]{:S(2)}, u32[]{:S(2)}) async-start(f32[16,64,128]{2,1,0:T(8,128)} %broadcast_in_dim.13), calls=%async_computation | async-start | bytes 1048576 | tf_op jit(solution)/shard_map/all_to_all | solution.py:218
  23.1 30.5 %all-to-all-start.3 = ((f32[16,64,128]{2,1,0:T(8,128)}), f32[16,64,128]{2,1,0:T(8,128)S(1)}, u32[]{:S(2)}, u32[]{:S(2)}) async-start(f32[16,64,128]{2,1,0:T(8,128)} %broadcast_in_dim.14), calls=%async_computation.3 | async-start | bytes 1048576 | tf_op jit(solution)/shard_map/all_to_all | solution.py:218
  27.5 1.6 copy-start.8
  29.1 1.6 copy-start.10
  30.7 1.6 copy-start.16
  49.6 2.0 copy-start
  51.5 2.0 copy-start.3
  53.6 51.4 %all-to-all-start.1 = ((f32[16,128,128]{2,1,0:T(8,128)}), f32[16,128,128]{2,1,0:T(8,128)S(1)}, u32[]{:S(2)}, u32[]{:S(2)}) async-start(f32[16,128,128]{2,1,0:T(8,128)} %states.1), calls=%async_computation.1 | async-start | bytes 2097152 | tf_op jit(solution)/shard_map/all_to_all | solution.py:218
  60.9 2.2 %copy-start.1 = (f32[8192,128]{1,0:T(8,128)S(1)}, f32[8192,128]{1,0:T(8,128)}, u32[]{:S(2)}) copy-start(f32[8192,128]{1,0:T(8,128)} %copy-done) | copy-start | bytes 12582916
  63.1 2.2 %copy-start.4 = (f32[8192,128]{1,0:T(8,128)S(1)}, f32[8192,128]{1,0:T(8,128)}, u32[]{:S(2)}) copy-start(f32[8192,128]{1,0:T(8,128)} %copy-done.3) | copy-start | bytes 12582916
  105.0 24.6 %all-to-all-start.4 = ((bf16[16,256,128]{2,1,0:T(8,128)(2,1)}), bf16[16,256,128]{2,1,0:T(8,128)(2,1)S(1)}, u32[]{:S(2)}, u32[]{:S(2)}) async-start(bf16[16,256,128]{2,1,0:T(8,128)(2,1)} %local_grads.1), calls=%async_computation.4 | async-start | bytes 2097152 | tf_op jit(solution)/shard_map/all_to_all | solution.py:218
  129.6 56.0 %all-to-all-start.2 = ((f32[16,128,128]{2,1,0:T(8,128)}), f32[16,128,128]{2,1,0:T(8,128)}, u32[]{:S(2)}, u32[]{:S(2)}) async-start(f32[16,128,128]{2,1,0:T(8,128)} %scan.1), calls=%async_computation.2 | async-start | bytes 2097152 | tf_op jit(solution)/shard_map/all_to_all | solution.py:218
  134.7 12.7 %collective-permute-start = (f32[128,128]{1,0:T(8,128)S(1)}, f32[128,128]{1,0:T(8,128)S(1)}, u32[]{:S(2)}, u32[]{:S(2)}) collective-permute-start(f32[128,128]{1,0:T(8,128)S(1)} %owner_grads.1), channel_id=1, source_target_pairs={{0,16},{16,0},{32,48},{48,32},{64,80},{80,64},{96,112},{112,96},{1... | collective-permute-start | bytes 196616 | tf_op jit(solution)/shard_map/ppermute | solution.py:291
  147.4 3.8 %collective-permute-start.1 = (f32[128,128]{1,0:T(8,128)S(1)}, f32[128,128]{1,0:T(8,128)S(1)}, u32[]{:S(2)}, u32[]{:S(2)}) collective-permute-start(f32[128,128]{1,0:T(8,128)S(1)} %add.9), channel_id=1, source_target_pairs={{0,32},{16,48},{32,0},{48,16},{64,96},{80,112},{96,64},{112,80},{1... | collective-permute-start | bytes 196616 | tf_op jit(solution)/shard_map/ppermute | solution.py:291
  151.2 33.1 %collective-permute-start.2 = (f32[128,128]{1,0:T(8,128)S(1)}, f32[128,128]{1,0:T(8,128)S(1)}, u32[]{:S(2)}, u32[]{:S(2)}) collective-permute-start(f32[128,128]{1,0:T(8,128)S(1)} %add.10), channel_id=1, source_target_pairs={{0,64},{16,80},{32,96},{48,112},{64,0},{80,16},{96,32},{112,48},{1... | collective-permute-start | bytes 196616 | tf_op jit(solution)/shard_map/ppermute | solution.py:291
  154.7 2.2 %copy-start.2 = (f32[8192,128]{1,0:T(8,128)S(1)}, f32[8192,128]{1,0:T(8,128)}, u32[]{:S(2)}) copy-start(f32[8192,128]{1,0:T(8,128)} %copy-done) | copy-start | bytes 12582916
  156.9 2.2 %copy-start.5 = (f32[8192,128]{1,0:T(8,128)S(1)}, f32[8192,128]{1,0:T(8,128)}, u32[]{:S(2)}) copy-start(f32[8192,128]{1,0:T(8,128)} %copy-done.3) | copy-start | bytes 12582916
  159.1 26.5 %copy-start.7 = (bf16[1,128,8192]{2,1,0:T(8,128)(2,1)S(1)}, bf16[1,128,8192]{2,1,0:T(8,128)(2,1)}, u32[]{:S(2)}) copy-start(bf16[1,128,8192]{2,1,0:T(8,128)(2,1)} %param.7) | copy-start | bytes 6291460
  180.4 2.0 copy-start.12
  182.3 2.0 copy-start.14
  185.6 1.6 copy-start.9
  187.2 1.6 copy-start.11
  188.8 2.2 %copy-start.13 = (f32[8192,128]{1,0:T(8,128)S(1)}, f32[8192,128]{1,0:T(8,128)}, u32[]{:S(2)}) copy-start(f32[8192,128]{1,0:T(8,128)} %copy-done.12) | copy-start | bytes 12582916
  191.0 2.2 %copy-start.15 = (f32[8192,128]{1,0:T(8,128)S(1)}, f32[8192,128]{1,0:T(8,128)}, u32[]{:S(2)}) copy-start(f32[8192,128]{1,0:T(8,128)} %copy-done.14) | copy-start | bytes 12582916

commit v2 on v0

v2 whole, which is shorter than its diff:
```python
import math

import jax
import jax.numpy as jnp
import ml_dtypes
import numpy as np
from jax import lax
from jax.experimental import pallas as pl
from jax.experimental.pallas import tpu as pltpu
from jax.sharding import PartitionSpec as P

HALF = 128
LEN = 256
STEPS = LEN // 8
MODES = 16
WIDTH = 512
BLOCKS = 8
TOGETHER = 4
PART = 256
F32 = jnp.float32
BF16 = jnp.bfloat16


def tables():
    angle = math.pi * np.outer(2 * np.arange(LEN) + 1, np.arange(LEN)) / (2 * LEN)
    forward = np.concatenate([np.cos(angle), -np.sin(angle)], 0)
    inverse = forward.T / LEN
    return forward.astype(ml_dtypes.bfloat16), inverse.astype(ml_dtypes.bfloat16)


def params(vmem=63):
    return pltpu.CompilerParams(vmem_limit_bytes=vmem * 1024 * 1024)


def cost(ops, moved):
    return pl.CostEstimate(flops=ops, bytes_accessed=moved, transcendentals=0)


def product(left, right):
    return (left.astype(F32) * right.astype(F32)).astype(BF16)


def total(terms):
    terms = list(terms)
    while len(terms) > 1:
        terms = [u + v for u, v in zip(terms[::2], terms[1::2])]
    return terms[0]


def copies_kernel(array, out):
    for d in range(out.shape[0]):
        out[d] = array[...]


def gate_kernel(core, keys, values, out_grad, queries, x_keep, g_keep, x_give, g_give):
    even = core[0] == 0
    for left, right, keep, give in ((keys, values, x_keep, x_give), (out_grad, queries, g_keep, g_give)):
        for q in range(keep.shape[1] // WIDTH):
            first = pl.ds(2 * q * WIDTH, WIDTH)
            second = pl.ds((2 * q + 1) * WIDTH, WIDTH)
            u = product(left[:, first], right[:, first])
            v = product(left[:, second], right[:, second])
            keep[:, pl.ds(q * WIDTH, WIDTH)] = jnp.where(even, u, v)
            give[:, pl.ds(q * WIDTH, WIDTH)] = jnp.where(even, v, u)


def ladder(width, flip=False):
    s = lax.broadcasted_iota(jnp.int32, (8, width), 0).astype(F32)
    return 7.0 - s if flip else s


def column(values):
    return jnp.sum(values, axis=0, keepdims=True)


def power_sums(rates, signals, lanes):
    y = [jnp.broadcast_to(jnp.exp(-8.0 * rate), (8, 128)) for rate in rates]
    power = list(y)

    def load(ref, back, k):
        return ref[pl.ds(LEN - 8 - 8 * k if back else 8 * k, 8), lanes]

    v = [[load(ref, back, 0)] * len(rates) for ref, back in signals]
    d = [list(u) for u in v]
    for k in range(1, STEPS):
        for i, (ref, back) in enumerate(signals):
            sk = load(ref, back, k)
            for j in range(len(rates)):
                v[i][j] = v[i][j] + power[j] * sk
                if k < STEPS - 1:
                    d[i][j] = d[i][j] + v[i][j]
        if k < STEPS - 1:
            power = [p * u for p, u in zip(power, y)]
    last = float(STEPS - 1)
    return [[(vj, last * vj - dj) for vj, dj in zip(vi, di)] for vi, di in zip(v, d)]


def state_kernel(core, prm, residue, x_keep, g_keep, x_got, g_got, x_out, g_out, sums, parts, x_s, g_s, sums_s):
    low = pl.multiple_of(core[0] * HALF, HALF)
    high = pl.multiple_of(HALF - core[0] * HALF, HALF)
    for keep, got, out, wide in ((x_keep, x_got, x_out, x_s), (g_keep, g_got, g_out, g_s)):
        for part, at in ((keep, low), (got, high)):
            block = part[...]
            out[pl.ds(at, HALF), :] = block
            wide[pl.ds(at, HALF), :] = block.astype(F32)
    for tile in range(WIDTH // 128):
        lanes = pl.ds(128 * tile, 128)
        s, r = ladder(128), ladder(128, True)

        def some(group, carry):
            modes = [TOGETHER * group + i for i in range(TOGETHER)]
            rates = [prm[0, pl.ds(m, 1), lanes] for m in modes]
            xs = power_sums(rates, ((x_s, True), (g_s, False)), lanes)
            for m, rate, (v, d) in zip(modes, rates, xs[0]):
                weight = jnp.exp(-rate * r)
                sums[0, pl.ds(m, 1), lanes] = column(weight * v)
                sums_s[pl.ds(m, 1), lanes] = column(weight * (8.0 * d + r * v))
            for m, rate, (v, d) in zip(modes, rates, xs[1]):
                weight = jnp.exp(-rate * s)
                sums[0, pl.ds(MODES + m, 1), lanes] = column(weight * v)
                sums_s[pl.ds(MODES + m, 1), lanes] = column(weight * (8.0 * d + s * v))
            return carry

        lax.fori_loop(0, MODES // TOGETHER, some, 0, unroll=True)
    parts[0] = sums_s[...].astype(BF16)
    sums[0, 2 * MODES : 3 * MODES, :] = residue[...]


def dft(table, signal):
    return jnp.dot(table, signal, preferred_element_type=F32)


def correlate(forward, inverse, left, right):
    lr, li, rr, ri = left[:LEN], left[LEN:], right[:LEN], right[LEN:]
    both = jnp.concatenate([(lr * rr + li * ri).astype(BF16), (lr * ri - li * rr).astype(BF16)], 0)
    return dft(inverse, both)


def convolve(forward, inverse, left, right):
    lr, li, rr, ri = left[:LEN], left[LEN:], right[:LEN], right[LEN:]
    both = jnp.concatenate([(lr * rr - li * ri).astype(BF16), (lr * ri + li * rr).astype(BF16)], 0)
    return dft(inverse, both)


def grad_kernel(prm, forward, inverse, x, g, parts, lag_s, sums_s):
    fwd, inv = forward[...], inverse[...]
    for part in range(WIDTH // PART):
        lanes = pl.ds(PART * part, PART)
        lag_s[:, lanes] = correlate(fwd, inv, dft(fwd, x[:, lanes]), dft(fwd, g[:, lanes]))
    for tile in range(WIDTH // 128):
        lanes = pl.ds(128 * tile, 128)
        s = ladder(128)

        def some(group, carry):
            modes = [TOGETHER * group + i for i in range(TOGETHER)]
            rates = [prm[0, pl.ds(m, 1), lanes] for m in modes]
            (lags,) = power_sums(rates, ((lag_s, False),), lanes)
            for m, rate, (v, d) in zip(modes, rates, lags):
                weight = jnp.exp(-rate * s)
                sums_s[pl.ds(m, 1), lanes] = column(weight * v)
                sums_s[pl.ds(MODES + m, 1), lanes] = column(weight * (8.0 * d + s * v))
            return carry

        lax.fori_loop(0, MODES // TOGETHER, some, 0, unroll=True)
    parts[0] = sums_s[...].astype(BF16)


def expand(rates, heads, flip, put):
    for tile in range(WIDTH // 128):
        lanes = slice(128 * tile, 128 * tile + 128)
        s = ladder(128, flip)
        y = tuple(jnp.broadcast_to(jnp.exp(-8.0 * rates[m : m + 1, lanes]), (8, 128)) for m in range(MODES))
        z = tuple(heads[m : m + 1, lanes] * jnp.exp(-rates[m : m + 1, lanes] * s) for m in range(MODES))
        for k in range(STEPS):
            put(k, lanes, total(z))
            if k < STEPS - 1:
                z = tuple(u * v for u, v in zip(z, y))


def local_kernel(prm, residue, forward, inverse, x, g, conv, back, filt_s):
    fwd, inv = forward[...], inverse[...]

    def put(k, lanes, rows):
        filt_s[pl.ds(8 * k, 8), lanes] = rows

    expand(prm[0], residue[0], False, put)
    for part in range(WIDTH // PART):
        lanes = pl.ds(PART * part, PART)
        filt = dft(fwd, filt_s[:, lanes].astype(BF16))
        conv[:, lanes] = convolve(fwd, inv, filt, dft(fwd, x[:, lanes]))
        back[:, lanes] = correlate(fwd, inv, filt, dft(fwd, g[:, lanes]))


def scan_kernel(sums, grad_a, grad_b, own_rate, residue, out):
    rate = own_rate[...]
    scale = residue[...] * jnp.exp(-rate)
    far = jnp.exp(-float(LEN) * rate)

    def write(d, base, state):
        ends = scale * state
        near = ends.astype(BF16)
        out[d, base : base + MODES, :] = near
        out[d, base + MODES : base + 2 * MODES, :] = (ends - near.astype(F32)).astype(BF16)

    state = jnp.zeros((MODES, WIDTH), F32)
    for d in range(BLOCKS):
        write(d, 0, state)
        state = far * state + sums[d, 0:MODES, :]
    state = jnp.zeros((MODES, WIDTH), F32)
    for d in range(BLOCKS - 1, -1, -1):
        write(d, 2 * MODES, state)
        state = far * state + sums[d, MODES : 2 * MODES, :]
    for d in range(BLOCKS):
        out[d, 64:96, :] = grad_a[d]
        out[d, 96:128, :] = grad_b[d]


def owner_grad_kernel(sums, got, own_rate, residue, out):
    rate = own_rate[...]
    lam = jnp.exp(-rate)
    far = jnp.exp(-float(LEN) * rate)
    zero = jnp.zeros((MODES, WIDTH), F32)
    h, q, hg, pg, hb, qb = zero, zero, zero, zero, zero, zero
    for d in range(BLOCKS):
        b = sums[d, MODES : 2 * MODES, :]
        p, w, hd, pd = (got[d, 64 + 16 * i : 80 + 16 * i, :].astype(F32) for i in range(4))
        hg = hg + hd
        pg = pg + pd
        hb = hb + h * b
        qb = qb + h * (w + b) + q * b
        q = far * (q + float(LEN) * h) + p
        h = far * h + sums[d, 0:MODES, :]
    first = hg + lam * hb
    second = -residue[...] * (pg + lam * qb)
    for b in range(out.shape[0]):
        out[b, 0:MODES, :] = first
        out[b, MODES : 2 * MODES, :] = second


def finish_kernel(core, prm, ends, conv, back, conv_keep, back_keep, conv_give, back_give, conv_s, back_s):
    rates = prm[0]
    head = ends[0, 0:16, :].astype(F32) + ends[0, 16:32, :].astype(F32)
    tail = ends[0, 32:48, :].astype(F32) + ends[0, 48:64, :].astype(F32)

    def put_conv(k, lanes, rows):
        at = pl.ds(8 * k, 8)
        conv_s[at, lanes] = conv[at, lanes] + rows

    def put_back(k, lanes, rows):
        at = pl.ds(LEN - 8 - 8 * k, 8)
        back_s[at, lanes] = back[at, lanes] + rows

    expand(rates, head, False, put_conv)
    expand(rates, tail, True, put_back)
    mine = pl.multiple_of(core[0] * HALF, HALF)
    other = pl.multiple_of(HALF - core[0] * HALF, HALF)
    for scratch, keep, give in ((conv_s, conv_keep, conv_give), (back_s, back_keep, back_give)):
        keep[...] = scratch[pl.ds(mine, HALF), :].astype(BF16)
        give[...] = scratch[pl.ds(other, HALF), :].astype(BF16)


def out_kernel(core, out_grad, keys, values, conv_keep, back_keep, conv_got, back_got, query_out, key_out, value_out):
    even = core[0] == 0
    for q in range(conv_keep.shape[1] // WIDTH):
        at = pl.ds(q * WIDTH, WIDTH)
        for h in range(2):
            lanes = pl.ds((2 * q + h) * WIDTH, WIDTH)
            c, b = (
                jnp.where(even, u[:, at], v[:, at]) if h == 0 else jnp.where(even, v[:, at], u[:, at])
                for u, v in ((conv_keep, conv_got), (back_keep, back_got))
            )
            query_out[:, lanes] = product(out_grad[:, lanes], c)
            key_out[:, lanes] = product(b, values[:, lanes])
            value_out[:, lanes] = product(b, keys[:, lanes])


def call(kernel, name, work, grid, in_specs, out_specs, shapes, scratch, operands, prefetch=True):
    spec = pltpu.PrefetchScalarGridSpec(
        num_scalar_prefetch=1 if prefetch else 0, grid=grid, in_specs=in_specs, out_specs=out_specs, scratch_shapes=scratch
    )
    return pl.pallas_call(
        kernel, grid_spec=spec, out_shape=shapes, compiler_params=params(), cost_estimate=work, name=name
    )(*operands)


def swap(array):
    return lax.ppermute(array, "ctx", [(i, i ^ 1) for i in range(2 * BLOCKS)])


def exchange(array):
    groups = [[2 * q + c for q in range(BLOCKS)] for c in range(2)]
    return lax.all_to_all(array, "ctx", split_axis=0, concat_axis=0, axis_index_groups=groups, tiled=True)


def body(queries, keys, values, out_grad, residue, rate):
    chans = queries.shape[2]
    half = chans // 2
    queries2, keys2, values2, out_grad2 = (a.reshape(HALF, chans) for a in (queries, keys, values, out_grad))
    core = (lax.axis_index("ctx") % 2).astype(jnp.int32).reshape(1)
    prm = exchange(
        pl.pallas_call(
            copies_kernel,
            out_shape=jax.ShapeDtypeStruct((BLOCKS, MODES, WIDTH), F32),
            compiler_params=params(),
            name="rate_copies",
        )(rate)
    )
    forward, inverse = tables()
    work = LEN * half * MODES
    moved = LEN * half

    part = pl.BlockSpec((HALF, WIDTH), lambda q, *_: (0, q))
    whole = pl.BlockSpec((LEN, WIDTH), lambda q, *_: (0, q))
    own = pl.BlockSpec((MODES, WIDTH), lambda q, *_: (0, 0))
    rows16 = pl.BlockSpec((1, MODES, WIDTH), lambda q, *_: (q, 0, 0))
    rows48 = pl.BlockSpec((1, 48, WIDTH), lambda q, *_: (q, 0, 0))
    residues = pl.BlockSpec((1, MODES, WIDTH), lambda q, *_: (q, 2, 0))
    rows32 = pl.BlockSpec((1, 32, WIDTH), lambda q, *_: (q, 0, 0))
    rows64 = pl.BlockSpec((1, 64, WIDTH), lambda q, *_: (q, 0, 0))
    table_f = pl.BlockSpec((2 * LEN, LEN), lambda q, *_: (0, 0))
    table_i = pl.BlockSpec((LEN, 2 * LEN), lambda q, *_: (0, 0))
    shape_part = jax.ShapeDtypeStruct((HALF, half), BF16)
    shape_whole = jax.ShapeDtypeStruct((LEN, half), BF16)
    shape_wide = jax.ShapeDtypeStruct((LEN, half), F32)
    shape_rows = jax.ShapeDtypeStruct((BLOCKS, 32, WIDTH), BF16)
    wide = pltpu.VMEM((LEN, WIDTH), F32)
    narrow = pltpu.VMEM((32, WIDTH), F32)

    pair = pl.BlockSpec((HALF, 4 * WIDTH), lambda q, *_: (0, q))
    pair_half = pl.BlockSpec((HALF, 2 * WIDTH), lambda q, *_: (0, q))
    x_keep, g_keep, x_give, g_give = call(
        gate_kernel, "gate", cost(2 * moved, 12 * moved), (BLOCKS // 2,), [pair] * 4, [pair_half] * 4, [shape_part] * 4, [],
        (core, keys2, values2, out_grad2, queries2),
    )
    x_give, g_give, prm = lax.optimization_barrier((x_give, g_give, prm))
    x_got, g_got = swap(x_give), swap(g_give)
    x, g, sums, grad_a = call(
        state_kernel, "states", cost(7 * work, 8 * moved), (BLOCKS,), [rows16, own] + [part] * 4,
        [whole, whole, rows48, rows32],
        [shape_whole, shape_whole, jax.ShapeDtypeStruct((BLOCKS, 48, WIDTH), F32), shape_rows],
        [wide, wide, narrow], (core, prm, residue, x_keep, g_keep, x_got, g_got),
    )
    sums_own = exchange(sums)
    grad_b = call(
        grad_kernel, "local_grads", cost(6 * work, 4 * moved), (BLOCKS,), [rows16, table_f, table_i, whole, whole],
        rows32, shape_rows, [wide, narrow], (prm, forward, inverse, x, g), False,
    )
    ends_own = pl.pallas_call(
        scan_kernel,
        out_shape=jax.ShapeDtypeStruct((BLOCKS, 128, WIDTH), BF16),
        compiler_params=params(),
        name="scan",
    )(sums_own, grad_a, grad_b, rate, residue)
    ends = exchange(ends_own)
    conv, back = call(
        local_kernel, "local_conv", cost(5 * work, 12 * moved), (BLOCKS,), [rows16, residues, table_f, table_i, whole, whole],
        [whole, whole], [shape_wide, shape_wide], [wide], (prm, sums_own, forward, inverse, x, g), False,
    )
    grads = pl.pallas_call(
        owner_grad_kernel,
        out_shape=jax.ShapeDtypeStruct((8, 32, WIDTH), F32),
        compiler_params=params(),
        name="owner_grads",
    )(sums_own, ends, rate, residue)
    grads, ends = lax.optimization_barrier((grads, ends))
    grads = lax.all_to_all(grads, "dp", split_axis=0, concat_axis=0, tiled=True)
    grads = jnp.sum(grads, 0)
    conv_keep, back_keep, conv_give, back_give = call(
        finish_kernel, "finish", cost(4 * work, 12 * moved), (BLOCKS,), [rows16, rows64, whole, whole], [part] * 4,
        [shape_part] * 4, [wide, wide], (core, prm, ends, conv, back),
    )
    conv_give, back_give, grads = lax.optimization_barrier((conv_give, back_give, grads))
    conv_got, back_got = swap(conv_give), swap(back_give)
    shape_out = jax.ShapeDtypeStruct((HALF, chans), BF16)
    outs = call(
        out_kernel, "outputs", cost(3 * moved, 16 * moved), (BLOCKS // 2,), [pair] * 3 + [pair_half] * 4, [pair] * 3,
        [shape_out] * 3, [], (core, out_grad2, keys2, values2, conv_keep, back_keep, conv_got, back_got),
    )
    query_grad, key_grad, value_grad = (a.reshape(queries.shape) for a in outs)
    return query_grad, key_grad, value_grad, grads[:MODES], grads[MODES:]


def solution(mesh):
    wide = P("dp", "ctx", None)
    narrow = P(None, "ctx")
    return jax.shard_map(
        body,
        mesh=mesh,
        in_specs=(wide,) * 4 + (narrow,) * 2,
        out_specs=(wide,) * 3 + (narrow,) * 2,
        check_vma=False,
    )
```

time: 651 us -> 145 us (0.22); the launches traced: 640 us -> 144 us
  local copies, waits for them, and re-layouts: 213 us -> 1.6 us
  other arithmetic: 169 us -> 0.04 us
  matrix products: 153 us -> 0 us
  Pallas kernels: 0 us -> 88.3 us
  blocking collectives: 42.9 us -> 22.8 us
  starting transfers between devices: 37.1 us -> 21.3 us
  loops' own time: 9.56 us -> 0 us
    dot_general x72 -> x0, matrix products: 153 us -> none  [narrow_einsum(): return jnp.einsum(form, left, right, preferred_element_type=jnp.float32)]
    unnamed x4 -> x0, other arithmetic: 120 us -> none
    pallas_call x0 -> x9, Pallas kernels: none -> 88.3 us  [the longest x6 82 us: call(): pl.pallas_call(kernel, grid_spec=spec, out_shape=shapes, compiler_params=...]
    unnamed x32 -> x4, local copies, waits for them, and re-layouts: 84.1 us -> 0.97 us
    convert_element_type x6 -> x0, local copies, waits for them, and re-layouts: 77.7 us -> none  [the longest x2 66.5 us: times_bf16(): (left.astype(jnp.float32) * right.astype(jnp.float32)).astype(jnp.bfloat16)]
    psum x1 -> x0, blocking collectives: 42.9 us -> none  [body(): lax.psum(res_local.astype(jnp.bfloat16), 'dp').astype(jnp.float32)]
    convert_element_type x12 -> x0, other arithmetic: 25.1 us -> none  [the longest x4 13.9 us: times_bf16(): (left.astype(jnp.float32) * right.astype(jnp.float32)).astype(jnp.bfloat16)]
    reduce_sum x2 -> x1, other arithmetic: 23.6 us -> 0.04 us  [body(): grads = jnp.sum(grads, 0)]
  transfers between devices with their start and end apart: 4 -> 7, of which waited for: 2 -> 5; matrix products, arithmetic and copies ran while one was open for 25% -> 0% of each run, Pallas kernels for 0% -> 38%
where the time goes in v2:
time: 145 us; the launch traced here: 144 us
  Pallas kernels  88.3 us (61%)
  blocking collectives  22.8 us (16%)
  starting transfers between devices  21.3 us (15%)
  waiting for transfers between devices  9.46 us (7%)
  local copies, waits for them, and re-layouts  1.6 us (1%)
    pallas_call x6, Pallas kernels, call(): pl.pallas_call(kernel, grid_spec=spec, out_shape=shapes, compiler_params=...  82 us
    all_to_all x1, blocking collectives, exchange(): lax.all_to_all(array, 'ctx', split_axis=0, concat_axis=0, axis_index_grou...  22.8 us
    all_to_all x2, starting transfers between devices, exchange(): lax.all_to_all(array, 'ctx', split_axis=0, concat_axis=0, axis_index_grou...  11.6 us
    ppermute x4, waiting for transfers between devices, swap(): return lax.ppermute(array, 'ctx', [(i, i ^ 1) for i in range(2 * BLOCKS)])  7.53 us
    all_to_all x1, starting transfers between devices, body(): grads = lax.all_to_all(grads, 'dp', split_axis=0, concat_axis=0, tiled=True)  5.15 us
    ppermute x4, starting transfers between devices, swap(): return lax.ppermute(array, 'ctx', [(i, i ^ 1) for i in range(2 * BLOCKS)])  4.55 us
  transfers between devices with their start and end apart: 7, of which 5 were waited for; matrix products, arithmetic and copies ran while one was open for 0% of the time, Pallas kernels for 38%

profile of v2, /device:TPU:1, one launch (start us, length us, event | category | flops | bytes accessed | tf_op | source)
XLA Modules:
  0.0 144.1 jit_solution(7777215362614099868)
XLA Ops:
  0.6 1.5 %rate_copies.1 = f32[8,16,512]{2,1,0:T(8,128)} custom-call(f32[16,512]{1,0:T(8,128)} %own_rate.3), custom_call_target="tpu_custom_call" | custom-call | tf_op jit(solution)/shard_map/rate_copies/pallas_call | solution.py:301
  2.1 7.5 %all-to-all-start = ((f32[8,16,512]{2,1,0:T(8,128)}), f32[8,16,512]{2,1,0:T(8,128)S(1)}, u32[]{:S(2)}, u32[]{:S(2)}) async-start(f32[8,16,512]{2,1,0:T(8,128)} %rate_copies.1), calls=%async_computation | async-start | bytes 524288 | tf_op jit(solution)/shard_map/all_to_all | solution.py:292
  9.6 5.9 %gate.1 = (bf16[128,4096]{1,0:T(8,128)(2,1)}, bf16[128,4096]{1,0:T(8,128)(2,1)}, bf16[128,4096]{1,0:T(8,128)(2,1)}, bf16[128,4096]{1,0:T(8,128)(2,1)}) custom-call(s32[1]{0:T(128)} %bitcast.core, bf16[128,8192]{1,0:T(8,128)(2,1)} %bitcast.10, bf16[128,8192]{1,0:T(8,128)(2,1)} %bitcast.12, bf16[128,8192]{1,0:T(8,128)(2,1)} %bitcast.8, bf16[128,8192]{1,0:T(8,128)(2,1)} %bitcast.14), custom_call_target="tpu_custom_call" | custom-call | flops 2097152 | bytes 12582912 | tf_op jit(solution)/shard_map/gate/pallas_call | solution.py:281
  15.5 1.9 %all-to-all-done.prm = f32[8,16,512]{2,1,0:T(8,128)S(1)} async-done(((f32[8,16,512]{2,1,0:T(8,128)}), f32[8,16,512]{2,1,0:T(8,128)S(1)}, u32[]{:S(2)}, u32[]{:S(2)}) %all-to-all-start) | async-done | bytes 262176 | tf_op jit(solution)/shard_map/all_to_all | solution.py:292
  17.4 0.0 copy-start.1
  17.4 1.9 %collective-permute-start = (bf16[128,4096]{1,0:T(8,128)(2,1)}, bf16[128,4096]{1,0:T(8,128)(2,1)}, u32[]{:S(2)}, u32[]{:S(2)}) collective-permute-start(bf16[128,4096]{1,0:T(8,128)(2,1)} %get-tuple-element.35), channel_id=1, source_target_pairs={{0,1},{1,0},{2,3},{3,2},{4,5},{5,4},{6,7},{7,6},{8,9},{9,8},{10,11... | collective-permute-start | bytes 3145736 | tf_op jit(solution)/shard_map/ppermute | solution.py:287
  19.4 0.0 collective-permute-start.1
  19.4 2.6 %collective-permute-done.x_got = bf16[128,4096]{1,0:T(8,128)(2,1)} collective-permute-done((bf16[128,4096]{1,0:T(8,128)(2,1)}, bf16[128,4096]{1,0:T(8,128)(2,1)}, u32[]{:S(2)}, u32[]{:S(2)}) %collective-permute-start) | collective-permute-done | bytes 1048608 | tf_op jit(solution)/shard_map/ppermute | solution.py:287
  22.0 1.5 %collective-permute-done.1.g_got = bf16[128,4096]{1,0:T(8,128)(2,1)} collective-permute-done((bf16[128,4096]{1,0:T(8,128)(2,1)}, bf16[128,4096]{1,0:T(8,128)(2,1)}, u32[]{:S(2)}, u32[]{:S(2)}) %collective-permute-start.1) | collective-permute-done | bytes 1048608 | tf_op jit(solution)/shard_map/ppermute | solution.py:287
  23.5 0.0 copy-done.1
  23.5 20.7 %states.1 = (bf16[256,4096]{1,0:T(8,128)(2,1)}, bf16[256,4096]{1,0:T(8,128)(2,1)}, f32[8,48,512]{2,1,0:T(8,128)}, bf16[8,32,512]{2,1,0:T(8,128)(2,1)}) custom-call(s32[1]{0:T(128)} %bitcast.core, f32[8,16,512]{2,1,0:T(8,128)} %copy-done.1, f32[16,512]{1,0:T(8,128)} %residue.5, bf16[128,4096]{1,0:T(8,128)(2,1)} %get-tuple-element.33.x_keep, ...), custom_call_target="tpu_custom_call" | custom-call | flops 117440512 | bytes 8388608 | tf_op jit(solution)/shard_map/states/pallas_call | solution.py:281
  44.2 4.1 %all-to-all-start.1 = ((f32[8,48,512]{2,1,0:T(8,128)}), f32[8,48,512]{2,1,0:T(8,128)S(1)}, u32[]{:S(2)}, u32[]{:S(2)}) async-start(f32[8,48,512]{2,1,0:T(8,128)} %get-tuple-element.37), calls=%async_computation.1 | async-start | bytes 1572864 | tf_op jit(solution)/shard_map/all_to_all | solution.py:292
  48.3 20.7 %local_grads.1.grad_b = bf16[8,32,512]{2,1,0:T(8,128)(2,1)} custom-call(f32[8,16,512]{2,1,0:T(8,128)} %copy-done.1, bf16[512,256]{1,0:T(8,128)(2,1)} %constant.23.clone.forward, bf16[256,512]{1,0:T(8,128)(2,1)} %constant.24.clone.inverse, bf16[256,4096]{1,0:T(8,128)(2,1)} %get-tuple-element.39.x, bf16[256,4096]{1,0:T(8,128)(2,1)} %get-tuple-element.40.g), custom_call_target="tpu_custom_call" | custom-call | flops 100663296 | bytes 4194304 | tf_op jit(solution)/shard_map/local_grads/pallas_call | solution.py:281
  68.9 0.0 all-to-all-done.1.sums.residue
  69.0 0.0 copy-start
  69.0 1.0 copy-done
  69.9 2.4 %scan.1 = bf16[8,128,512]{2,1,0:T(8,128)(2,1)} custom-call(f32[8,48,512]{2,1,0:T(8,128)} %copy-done, bf16[8,32,512]{2,1,0:T(8,128)(2,1)} %get-tuple-element.38.grad_a, bf16[8,32,512]{2,1,0:T(8,128)(2,1)} %local_grads.1.grad_b, f32[16,512]{1,0:T(8,128)} %own_rate.3, f32[16,512]{1,0:T(8,128)} %residue.5), custom_call_target="tpu_custom_call" | custom-call | tf_op jit(solution)/shard_map/scan/pallas_call | solution.py:348
  72.3 22.8 %all_to_all.20.got.ends = bf16[8,128,512]{2,1,0:T(8,128)(2,1)} all-to-all(bf16[8,128,512]{2,1,0:T(8,128)(2,1)} %scan.1), channel_id=1, replica_groups={{0,2,4,6,8,10,12,14},{1,3,5,7,9,11,13,15},{16,18,20,22,24,26,28,30},{17..., dimensions={0} | all-to-all | bytes 2097152 | tf_op jit(solution)/shard_map/all_to_all | solution.py:292
  95.1 2.4 %owner_grads.1 = f32[8,32,512]{2,1,0:T(8,128)} custom-call(f32[8,48,512]{2,1,0:T(8,128)} %copy-done, bf16[8,128,512]{2,1,0:T(8,128)(2,1)} %all_to_all.20.got.ends, f32[16,512]{1,0:T(8,128)} %own_rate.3, f32[16,512]{1,0:T(8,128)} %residue.5), custom_call_target="tpu_custom_call" | custom-call | tf_op jit(solution)/shard_map/owner_grads/pallas_call | solution.py:359
  97.5 5.1 %all-to-all-start.3 = ((f32[8,32,512]{2,1,0:T(8,128)}), f32[8,32,512]{2,1,0:T(8,128)S(1)}, u32[]{:S(2)}, u32[]{:S(2)}) async-start(f32[8,32,512]{2,1,0:T(8,128)} %owner_grads.1), calls=%async_computation.3 | async-start | bytes 1048576 | tf_op jit(solution)/shard_map/all_to_all | solution.py:366
  102.6 15.6 %local_conv.1 = (f32[256,4096]{1,0:T(8,128)}, f32[256,4096]{1,0:T(8,128)}) custom-call(f32[8,16,512]{2,1,0:T(8,128)} %copy-done.1, f32[8,48,512]{2,1,0:T(8,128)} %copy-done, bf16[512,256]{1,0:T(8,128)(2,1)} %constant.23.clone.forward, bf16[256,512]{1,0:T(8,128)(2,1)} %constant.24.clone.inverse, bf16[256,4096]{1,0:T(8,128)(2,1)} %get-tuple-element.39.x, ...), custom_call_target="tpu_custom_call" | custom-call | flops 83886080 | bytes 12582912 | tf_op jit(solution)/shard_map/local_conv/pallas_call | solution.py:281
  118.2 12.4 %finish.1 = (bf16[128,4096]{1,0:T(8,128)(2,1)}, bf16[128,4096]{1,0:T(8,128)(2,1)}, bf16[128,4096]{1,0:T(8,128)(2,1)}, bf16[128,4096]{1,0:T(8,128)(2,1)}) custom-call(s32[1]{0:T(128)} %bitcast.core, f32[8,16,512]{2,1,0:T(8,128)} %copy-done.1, bf16[8,128,512]{2,1,0:T(8,128)(2,1)} %all_to_all.20.got.ends, f32[256,4096]{1,0:T(8,128)} %get-tuple-element.42.conv, ...), custom_call_target="tpu_custom_call" | custom-call | flops 67108864 | bytes 12582912 | tf_op jit(solution)/shard_map/finish/pallas_call | solution.py:281
  130.6 0.0 all-to-all-done.3
  130.6 2.5 %collective-permute-start.2 = (bf16[128,4096]{1,0:T(8,128)(2,1)}, bf16[128,4096]{1,0:T(8,128)(2,1)}, u32[]{:S(2)}, u32[]{:S(2)}) collective-permute-start(bf16[128,4096]{1,0:T(8,128)(2,1)} %get-tuple-element.49), channel_id=1, source_target_pairs={{0,1},{1,0},{2,3},{3,2},{4,5},{5,4},{6,7},{7,6},{8,9},{9,8},{10,11... | collective-permute-start | bytes 3145736 | tf_op jit(solution)/shard_map/ppermute | solution.py:287
  133.1 0.1 collective-permute-start.3
  133.2 0.6 fusion
  133.9 1.9 %collective-permute-done.2.conv_got = bf16[128,4096]{1,0:T(8,128)(2,1)} collective-permute-done((bf16[128,4096]{1,0:T(8,128)(2,1)}, bf16[128,4096]{1,0:T(8,128)(2,1)}, u32[]{:S(2)}, u32[]{:S(2)}) %collective-permute-start.2) | collective-permute-done | bytes 1048608 | tf_op jit(solution)/shard_map/ppermute | solution.py:287
  135.8 1.5 %collective-permute-done.3.back_got = bf16[128,4096]{1,0:T(8,128)(2,1)} collective-permute-done((bf16[128,4096]{1,0:T(8,128)(2,1)}, bf16[128,4096]{1,0:T(8,128)(2,1)}, u32[]{:S(2)}, u32[]{:S(2)}) %collective-permute-start.3) | collective-permute-done | bytes 1048608 | tf_op jit(solution)/shard_map/ppermute | solution.py:287
  137.3 6.8 %outputs.1 = (bf16[128,8192]{1,0:T(8,128)(2,1)}, bf16[128,8192]{1,0:T(8,128)(2,1)}, bf16[128,8192]{1,0:T(8,128)(2,1)}) custom-call(s32[1]{0:T(128)} %bitcast.core, bf16[128,8192]{1,0:T(8,128)(2,1)} %bitcast.9, bf16[128,8192]{1,0:T(8,128)(2,1)} %bitcast.11, bf16[128,8192]{1,0:T(8,128)(2,1)} %bitcast.13, bf16[128,4096]{1,0:T(8,128)(2,1)} %get-tuple-element.44.conv_keep, ...), custom_call_target="tpu_custom_call" | custom-call | flops 3145728 | bytes 16777216 | tf_op jit(solution)/shard_map/outputs/pallas_call | solution.py:281
  (1 shorter events, 0.0 us)
Async XLA Ops:
  2.1 15.3 %all-to-all-start = ((f32[8,16,512]{2,1,0:T(8,128)}), f32[8,16,512]{2,1,0:T(8,128)S(1)}, u32[]{:S(2)}, u32[]{:S(2)}) async-start(f32[8,16,512]{2,1,0:T(8,128)} %rate_copies.1), calls=%async_computation | async-start | bytes 524288 | tf_op jit(solution)/shard_map/all_to_all | solution.py:292
  17.4 6.1 %copy-start.1 = (f32[8,16,512]{2,1,0:T(8,128)}, f32[8,16,512]{2,1,0:T(8,128)S(1)}, u32[]{:S(2)}) copy-start(f32[8,16,512]{2,1,0:T(8,128)S(1)} %all-to-all-done.prm) | copy-start | bytes 786436
  17.4 4.6 %collective-permute-start = (bf16[128,4096]{1,0:T(8,128)(2,1)}, bf16[128,4096]{1,0:T(8,128)(2,1)}, u32[]{:S(2)}, u32[]{:S(2)}) collective-permute-start(bf16[128,4096]{1,0:T(8,128)(2,1)} %get-tuple-element.35), channel_id=1, source_target_pairs={{0,1},{1,0},{2,3},{3,2},{4,5},{5,4},{6,7},{7,6},{8,9},{9,8},{10,11... | collective-permute-start | bytes 3145736 | tf_op jit(solution)/shard_map/ppermute | solution.py:287
  19.4 4.1 %collective-permute-start.1 = (bf16[128,4096]{1,0:T(8,128)(2,1)}, bf16[128,4096]{1,0:T(8,128)(2,1)}, u32[]{:S(2)}, u32[]{:S(2)}) collective-permute-start(bf16[128,4096]{1,0:T(8,128)(2,1)} %get-tuple-element.36), channel_id=1, source_target_pairs={{0,1},{1,0},{2,3},{3,2},{4,5},{5,4},{6,7},{7,6},{8,9},{9,8},{10,11... | collective-permute-start | bytes 3145736 | tf_op jit(solution)/shard_map/ppermute | solution.py:287
  44.2 24.8 %all-to-all-start.1 = ((f32[8,48,512]{2,1,0:T(8,128)}), f32[8,48,512]{2,1,0:T(8,128)S(1)}, u32[]{:S(2)}, u32[]{:S(2)}) async-start(f32[8,48,512]{2,1,0:T(8,128)} %get-tuple-element.37), calls=%async_computation.1 | async-start | bytes 1572864 | tf_op jit(solution)/shard_map/all_to_all | solution.py:292
  69.0 1.0 copy-start
  97.5 33.1 %all-to-all-start.3 = ((f32[8,32,512]{2,1,0:T(8,128)}), f32[8,32,512]{2,1,0:T(8,128)S(1)}, u32[]{:S(2)}, u32[]{:S(2)}) async-start(f32[8,32,512]{2,1,0:T(8,128)} %owner_grads.1), calls=%async_computation.3 | async-start | bytes 1048576 | tf_op jit(solution)/shard_map/all_to_all | solution.py:366
  130.6 5.1 %collective-permute-start.2 = (bf16[128,4096]{1,0:T(8,128)(2,1)}, bf16[128,4096]{1,0:T(8,128)(2,1)}, u32[]{:S(2)}, u32[]{:S(2)}) collective-permute-start(bf16[128,4096]{1,0:T(8,128)(2,1)} %get-tuple-element.49), channel_id=1, source_target_pairs={{0,1},{1,0},{2,3},{3,2},{4,5},{5,4},{6,7},{7,6},{8,9},{9,8},{10,11... | collective-permute-start | bytes 3145736 | tf_op jit(solution)/shard_map/ppermute | solution.py:287
  133.1 4.1 %collective-permute-start.3 = (bf16[128,4096]{1,0:T(8,128)(2,1)}, bf16[128,4096]{1,0:T(8,128)(2,1)}, u32[]{:S(2)}, u32[]{:S(2)}) collective-permute-start(bf16[128,4096]{1,0:T(8,128)(2,1)} %get-tuple-element.50), channel_id=1, source_target_pairs={{0,1},{1,0},{2,3},{3,2},{4,5},{5,4},{6,7},{7,6},{8,9},{9,8},{10,11... | collective-permute-start | bytes 3145736 | tf_op jit(solution)/shard_map/ppermute | solution.py:287

commit v3 on v2

--- a/solution.py
+++ b/solution.py
@@ -165,30 +165,37 @@
     parts[0] = sums_s[...].astype(BF16)
 
 
-def expand(rates, heads, flip, put):
+def expand(minus, steps, heads, flip, put, count):
     for tile in range(WIDTH // 128):
-        lanes = slice(128 * tile, 128 * tile + 128)
+        lanes = pl.ds(128 * tile, 128)
         s = ladder(128, flip)
-        y = tuple(jnp.broadcast_to(jnp.exp(-8.0 * rates[m : m + 1, lanes]), (8, 128)) for m in range(MODES))
-        z = tuple(heads[m : m + 1, lanes] * jnp.exp(-rates[m : m + 1, lanes] * s) for m in range(MODES))
-        for k in range(STEPS):
+        y = tuple(jnp.broadcast_to(steps[pl.ds(m, 1), lanes], (8, 128)) for m in range(MODES))
+        z = tuple(heads[pl.ds(m, 1), lanes] * jnp.exp(minus[pl.ds(m, 1), lanes] * s) for m in range(MODES))
+        for k in range(count):
             put(k, lanes, total(z))
-            if k < STEPS - 1:
+            if k < count - 1:
                 z = tuple(u * v for u, v in zip(z, y))
 
 
-def local_kernel(prm, residue, forward, inverse, x, g, conv, back, filt_s):
+def local_kernel(core, prm, residue, forward, inverse, x, g, conv_keep, back_keep, conv_give, back_give, filt_s, minus_s, step_s, res_s):
     fwd, inv = forward[...], inverse[...]
+    even = core[0] == 0
+    minus_s[...] = -prm[0]
+    step_s[...] = jnp.exp(-8.0 * prm[0])
+    res_s[...] = residue[0]
 
     def put(k, lanes, rows):
         filt_s[pl.ds(8 * k, 8), lanes] = rows
 
-    expand(prm[0], residue[0], False, put)
+    expand(minus_s, step_s, res_s, False, put, STEPS)
     for part in range(WIDTH // PART):
         lanes = pl.ds(PART * part, PART)
         filt = dft(fwd, filt_s[:, lanes].astype(BF16))
-        conv[:, lanes] = convolve(fwd, inv, filt, dft(fwd, x[:, lanes]))
-        back[:, lanes] = correlate(fwd, inv, filt, dft(fwd, g[:, lanes]))
+        conv = convolve(fwd, inv, filt, dft(fwd, x[:, lanes])).astype(BF16)
+        back = correlate(fwd, inv, filt, dft(fwd, g[:, lanes])).astype(BF16)
+        for both, keep, give in ((conv, conv_keep, conv_give), (back, back_keep, back_give)):
+            keep[:, lanes] = jnp.where(even, both[:HALF], both[HALF:])
+            give[:, lanes] = jnp.where(even, both[HALF:], both[:HALF])
 
 
 def scan_kernel(sums, grad_a, grad_b, own_rate, residue, out):
@@ -223,7 +230,7 @@
     h, q, hg, pg, hb, qb = zero, zero, zero, zero, zero, zero
     for d in range(BLOCKS):
         b = sums[d, MODES : 2 * MODES, :]
-        p, w, hd, pd = (got[d, 64 + 16 * i : 80 + 16 * i, :].astype(F32) for i in range(4))
+        p, w, hd, pd = (got[d, 16 * i : 16 * i + 16, :].astype(F32) for i in range(4))
         hg = hg + hd
         pg = pg + pd
         hb = hb + h * b
@@ -237,41 +244,34 @@
         out[b, MODES : 2 * MODES, :] = second
 
 
-def finish_kernel(core, prm, ends, conv, back, conv_keep, back_keep, conv_give, back_give, conv_s, back_s):
-    rates = prm[0]
-    head = ends[0, 0:16, :].astype(F32) + ends[0, 16:32, :].astype(F32)
-    tail = ends[0, 32:48, :].astype(F32) + ends[0, 48:64, :].astype(F32)
-
-    def put_conv(k, lanes, rows):
-        at = pl.ds(8 * k, 8)
-        conv_s[at, lanes] = conv[at, lanes] + rows
-
-    def put_back(k, lanes, rows):
-        at = pl.ds(LEN - 8 - 8 * k, 8)
-        back_s[at, lanes] = back[at, lanes] + rows
-
-    expand(rates, head, False, put_conv)
-    expand(rates, tail, True, put_back)
-    mine = pl.multiple_of(core[0] * HALF, HALF)
-    other = pl.multiple_of(HALF - core[0] * HALF, HALF)
-    for scratch, keep, give in ((conv_s, conv_keep, conv_give), (back_s, back_keep, back_give)):
-        keep[...] = scratch[pl.ds(mine, HALF), :].astype(BF16)
-        give[...] = scratch[pl.ds(other, HALF), :].astype(BF16)
-
-
-def out_kernel(core, out_grad, keys, values, conv_keep, back_keep, conv_got, back_got, query_out, key_out, value_out):
-    even = core[0] == 0
-    for q in range(conv_keep.shape[1] // WIDTH):
-        at = pl.ds(q * WIDTH, WIDTH)
-        for h in range(2):
-            lanes = pl.ds((2 * q + h) * WIDTH, WIDTH)
-            c, b = (
-                jnp.where(even, u[:, at], v[:, at]) if h == 0 else jnp.where(even, v[:, at], u[:, at])
-                for u, v in ((conv_keep, conv_got), (back_keep, back_got))
-            )
-            query_out[:, lanes] = product(out_grad[:, lanes], c)
-            key_out[:, lanes] = product(b, values[:, lanes])
-            value_out[:, lanes] = product(b, keys[:, lanes])
+def finish_kernel(
+    core, prm, prm_got, ends, ends_got, conv_keep, back_keep, conv_got, back_got, out_grad, keys, values,
+    query_out, key_out, value_out, minus_s, step_s, head_s, tail_s, conv_s, back_s,
+):
+    upper = core[0].astype(F32) * float(HALF)
+    for h in range(2):
+        mine = core[0] == h
+        minus = -jnp.where(mine, prm[0], prm_got[0])
+        edge = jnp.where(mine, ends[0], ends_got[0]).astype(F32)
+        minus_s[h] = minus
+        step_s[h] = jnp.exp(8.0 * minus)
+        head_s[h] = (edge[0:16] + edge[16:32]) * jnp.exp(minus * upper)
+        tail_s[h] = (edge[32:48] + edge[48:64]) * jnp.exp(minus * (float(HALF) - upper))
+
+        def put_conv(k, lanes, rows):
+            conv_s[h, pl.ds(8 * k, 8), lanes] = rows
+
+        def put_back(k, lanes, rows):
+            back_s[h, pl.ds(HALF - 8 - 8 * k, 8), lanes] = rows
+
+        expand(minus_s.at[h], step_s.at[h], head_s.at[h], False, put_conv, HALF // 8)
+        expand(minus_s.at[h], step_s.at[h], tail_s.at[h], True, put_back, HALF // 8)
+        c = (jnp.where(mine, conv_keep[...], conv_got[...]).astype(F32) + conv_s[h]).astype(BF16)
+        b = (jnp.where(mine, back_keep[...], back_got[...]).astype(F32) + back_s[h]).astype(BF16)
+        lanes = pl.ds(h * WIDTH, WIDTH)
+        query_out[:, lanes] = product(out_grad[:, lanes], c)
+        key_out[:, lanes] = product(b, values[:, lanes])
+        value_out[:, lanes] = product(b, keys[:, lanes])
 
 
 def call(kernel, name, work, grid, in_specs, out_specs, shapes, scratch, operands, prefetch=True):
@@ -321,7 +321,6 @@
     table_i = pl.BlockSpec((LEN, 2 * LEN), lambda q, *_: (0, 0))
     shape_part = jax.ShapeDtypeStruct((HALF, half), BF16)
     shape_whole = jax.ShapeDtypeStruct((LEN, half), BF16)
-    shape_wide = jax.ShapeDtypeStruct((LEN, half), F32)
     shape_rows = jax.ShapeDtypeStruct((BLOCKS, 32, WIDTH), BF16)
     wide = pltpu.VMEM((LEN, WIDTH), F32)
     narrow = pltpu.VMEM((32, WIDTH), F32)
@@ -333,7 +332,7 @@
         (core, keys2, values2, out_grad2, queries2),
     )
     x_give, g_give, prm = lax.optimization_barrier((x_give, g_give, prm))
-    x_got, g_got = swap(x_give), swap(g_give)
+    x_got, g_got, prm_got = swap(x_give), swap(g_give), swap(prm)
     x, g, sums, grad_a = call(
         state_kernel, "states", cost(7 * work, 8 * moved), (BLOCKS,), [rows16, own] + [part] * 4,
         [whole, whole, rows48, rows32],
@@ -341,6 +340,7 @@
         [wide, wide, narrow], (core, prm, residue, x_keep, g_keep, x_got, g_got),
     )
     sums_own = exchange(sums)
+    prm_got, x = lax.optimization_barrier((prm_got, x))
     grad_b = call(
         grad_kernel, "local_grads", cost(6 * work, 4 * moved), (BLOCKS,), [rows16, table_f, table_i, whole, whole],
         rows32, shape_rows, [wide, narrow], (prm, forward, inverse, x, g), False,
@@ -352,30 +352,36 @@
         name="scan",
     )(sums_own, grad_a, grad_b, rate, residue)
     ends = exchange(ends_own)
-    conv, back = call(
-        local_kernel, "local_conv", cost(5 * work, 12 * moved), (BLOCKS,), [rows16, residues, table_f, table_i, whole, whole],
-        [whole, whole], [shape_wide, shape_wide], [wide], (prm, sums_own, forward, inverse, x, g), False,
-    )
-    grads = pl.pallas_call(
-        owner_grad_kernel,
-        out_shape=jax.ShapeDtypeStruct((8, 32, WIDTH), F32),
-        compiler_params=params(),
-        name="owner_grads",
-    )(sums_own, ends, rate, residue)
+    few = pltpu.VMEM((MODES, WIDTH), F32)
+    conv_keep, back_keep, conv_give, back_give = call(
+        local_kernel, "local_conv", cost(5 * work, 8 * moved), (BLOCKS,),
+        [rows16, residues, table_f, table_i, whole, whole], [part] * 4, [shape_part] * 4, [wide] + [few] * 3,
+        (core, prm, sums_own, forward, inverse, x, g),
+    )
+    conv_got, back_got = swap(conv_give), swap(back_give)
+    ends, conv_keep = lax.optimization_barrier((ends, conv_keep))
+    ends_got = swap(ends)
+    owned = lambda rows, i=0: pl.BlockSpec((BLOCKS, rows, WIDTH), lambda *_: (0, i, 0))
+    grads = call(
+        owner_grad_kernel, "owner_grads", cost(1000, 2000000), (1,), [owned(32), owned(64, 1), own, own],
+        pl.BlockSpec((8, 32, WIDTH), lambda *_: (0, 0, 0)), jax.ShapeDtypeStruct((8, 32, WIDTH), F32), [],
+        (sums_own, ends, rate, residue), False,
+    )
     grads, ends = lax.optimization_barrier((grads, ends))
     grads = lax.all_to_all(grads, "dp", split_axis=0, concat_axis=0, tiled=True)
+    big = pl.BlockSpec((HALF, 2 * WIDTH), lambda q, *_: (0, q))
+    pair_specs = [rows16, rows16, rows64, rows64]
+    shape_out = jax.ShapeDtypeStruct((HALF, chans), BF16)
+    half_wide = pltpu.VMEM((2, HALF, WIDTH), F32)
+    few_two = pltpu.VMEM((2, MODES, WIDTH), F32)
+    outs = call(
+        finish_kernel, "finish", cost(4 * work, 20 * moved), (BLOCKS,),
+        pair_specs + [part] * 4 + [big] * 3, [big] * 3, [shape_out] * 3,
+        [few_two] * 4 + [half_wide] * 2,
+        (core, prm, prm_got, ends, ends_got, conv_keep, back_keep, conv_got, back_got, out_grad2, keys2, values2),
+    )
+    outs, grads = lax.optimization_barrier((outs, grads))
     grads = jnp.sum(grads, 0)
-    conv_keep, back_keep, conv_give, back_give = call(
-        finish_kernel, "finish", cost(4 * work, 12 * moved), (BLOCKS,), [rows16, rows64, whole, whole], [part] * 4,
-        [shape_part] * 4, [wide, wide], (core, prm, ends, conv, back),
-    )
-    conv_give, back_give, grads = lax.optimization_barrier((conv_give, back_give, grads))
-    conv_got, back_got = swap(conv_give), swap(back_give)
-    shape_out = jax.ShapeDtypeStruct((HALF, chans), BF16)
-    outs = call(
-        out_kernel, "outputs", cost(3 * moved, 16 * moved), (BLOCKS // 2,), [pair] * 3 + [pair_half] * 4, [pair] * 3,
-        [shape_out] * 3, [], (core, out_grad2, keys2, values2, conv_keep, back_keep, conv_got, back_got),
-    )
     query_grad, key_grad, value_grad = (a.reshape(queries.shape) for a in outs)
     return query_grad, key_grad, value_grad, grads[:MODES], grads[MODES:]
 

time: 145 us -> 124 us (0.86)
  blocking collectives: 22.8 us -> 0 us
  starting transfers between devices: 21.3 us -> 27.8 us
  Pallas kernels: 88.3 us -> 83.7 us
    all_to_all x1 -> x0, blocking collectives: 22.8 us -> none  [exchange(): lax.all_to_all(array, 'ctx', split_axis=0, concat_axis=0, axis_index_grou...]
    all_to_all x2 -> x3, starting transfers between devices: 11.6 us -> 18.5 us  [exchange(): lax.all_to_all(array, 'ctx', split_axis=0, concat_axis=0, axis_index_grou...]
    pallas_call x1 -> x0, Pallas kernels: 2.42 us -> none  [body(): pl.pallas_call(owner_grad_kernel, out_shape=jax.ShapeDtypeStruct((8, 32,...]
    pallas_call x6, Pallas kernels: 82 us -> 79.8 us  [call(): pl.pallas_call(kernel, grid_spec=spec, out_shape=shapes, compiler_params=...]
    ppermute x4 -> x6, waiting for transfers between devices: 7.53 us -> 5.64 us  [swap(): return lax.ppermute(array, 'ctx', [(i, i ^ 1) for i in range(2 * BLOCKS)])]
    all_to_all x2 -> x3, waiting for transfers between devices: 1.93 us -> 3.34 us  [exchange(): lax.all_to_all(array, 'ctx', split_axis=0, concat_axis=0, axis_index_grou...]
    ppermute x4 -> x6, starting transfers between devices: 4.55 us -> 4.19 us  [swap(): return lax.ppermute(array, 'ctx', [(i, i ^ 1) for i in range(2 * BLOCKS)])]
  transfers between devices with their start and end apart: 7 -> 10, of which waited for: 5 -> 5; matrix products, arithmetic and copies ran while one was open for 0% -> 0% of each run, Pallas kernels for 38% -> 48%
where the time goes in v3:
time: 124 us; the launch traced here: 123 us
  Pallas kernels  83.7 us (68%)
  starting transfers between devices  27.8 us (22%)
  waiting for transfers between devices  8.98 us (7%)
  local copies, waits for them, and re-layouts  1.61 us (1%)
    pallas_call x6, Pallas kernels, call(): pl.pallas_call(kernel, grid_spec=spec, out_shape=shapes, compiler_params=...  79.8 us
    all_to_all x3, starting transfers between devices, exchange(): lax.all_to_all(array, 'ctx', split_axis=0, concat_axis=0, axis_index_grou...  18.5 us
    ppermute x6, waiting for transfers between devices, swap(): return lax.ppermute(array, 'ctx', [(i, i ^ 1) for i in range(2 * BLOCKS)])  5.64 us
    all_to_all x1, starting transfers between devices, body(): grads = lax.all_to_all(grads, 'dp', split_axis=0, concat_axis=0, tiled=True)  5.13 us
    ppermute x6, starting transfers between devices, swap(): return lax.ppermute(array, 'ctx', [(i, i ^ 1) for i in range(2 * BLOCKS)])  4.19 us
    all_to_all x3, waiting for transfers between devices, exchange(): lax.all_to_all(array, 'ctx', split_axis=0, concat_axis=0, axis_index_grou...  3.34 us
  transfers between devices with their start and end apart: 10, of which 5 were waited for; matrix products, arithmetic and copies ran while one was open for 0% of the time, Pallas kernels for 48%

profile of v3, /device:TPU:1, one launch (start us, length us, event | category | flops | bytes accessed | tf_op | source)
XLA Modules:
  0.0 122.9 jit_solution(13059694315726778753)
XLA Ops:
  0.6 1.5 %rate_copies.1 = f32[8,16,512]{2,1,0:T(8,128)} custom-call(f32[16,512]{1,0:T(8,128)} %own_rate.3), custom_call_target="tpu_custom_call" | custom-call | tf_op jit(solution)/shard_map/rate_copies/pallas_call | solution.py:301
  2.1 7.5 %all-to-all-start = ((f32[8,16,512]{2,1,0:T(8,128)}), f32[8,16,512]{2,1,0:T(8,128)S(1)}, u32[]{:S(2)}, u32[]{:S(2)}) async-start(f32[8,16,512]{2,1,0:T(8,128)} %rate_copies.1), calls=%async_computation | async-start | bytes 524288 | tf_op jit(solution)/shard_map/all_to_all | solution.py:292
  9.6 5.9 %gate.1 = (bf16[128,4096]{1,0:T(8,128)(2,1)}, bf16[128,4096]{1,0:T(8,128)(2,1)}, bf16[128,4096]{1,0:T(8,128)(2,1)}, bf16[128,4096]{1,0:T(8,128)(2,1)}) custom-call(s32[1]{0:T(128)} %bitcast.core, bf16[128,8192]{1,0:T(8,128)(2,1)} %bitcast.8, bf16[128,8192]{1,0:T(8,128)(2,1)} %bitcast.10, bf16[128,8192]{1,0:T(8,128)(2,1)} %bitcast.12, bf16[128,8192]{1,0:T(8,128)(2,1)} %bitcast.14), custom_call_target="tpu_custom_call" | custom-call | flops 2097152 | bytes 12582912 | tf_op jit(solution)/shard_map/gate/pallas_call | solution.py:281
  15.5 1.9 %all-to-all-done.prm = f32[8,16,512]{2,1,0:T(8,128)S(1)} async-done(((f32[8,16,512]{2,1,0:T(8,128)}), f32[8,16,512]{2,1,0:T(8,128)S(1)}, u32[]{:S(2)}, u32[]{:S(2)}) %all-to-all-start) | async-done | bytes 262176 | tf_op jit(solution)/shard_map/all_to_all | solution.py:292
  17.4 0.0 copy-start.1
  17.4 1.9 %collective-permute-start.1 = (bf16[128,4096]{1,0:T(8,128)(2,1)}, bf16[128,4096]{1,0:T(8,128)(2,1)}, u32[]{:S(2)}, u32[]{:S(2)}) collective-permute-start(bf16[128,4096]{1,0:T(8,128)(2,1)} %get-tuple-element.38), channel_id=1, source_target_pairs={{0,1},{1,0},{2,3},{3,2},{4,5},{5,4},{6,7},{7,6},{8,9},{9,8},{10,11... | collective-permute-start | bytes 3145736 | tf_op jit(solution)/shard_map/ppermute | solution.py:287
  19.3 0.0 collective-permute-start.2
  19.3 2.6 %collective-permute-done.1.x_got = bf16[128,4096]{1,0:T(8,128)(2,1)} collective-permute-done((bf16[128,4096]{1,0:T(8,128)(2,1)}, bf16[128,4096]{1,0:T(8,128)(2,1)}, u32[]{:S(2)}, u32[]{:S(2)}) %collective-permute-start.1) | collective-permute-done | bytes 1048608 | tf_op jit(solution)/shard_map/ppermute | solution.py:287
  22.0 1.5 %collective-permute-done.2.g_got = bf16[128,4096]{1,0:T(8,128)(2,1)} collective-permute-done((bf16[128,4096]{1,0:T(8,128)(2,1)}, bf16[128,4096]{1,0:T(8,128)(2,1)}, u32[]{:S(2)}, u32[]{:S(2)}) %collective-permute-start.2) | collective-permute-done | bytes 1048608 | tf_op jit(solution)/shard_map/ppermute | solution.py:287
  23.5 0.0 copy-done.1
  23.5 20.7 %states.1 = (bf16[256,4096]{1,0:T(8,128)(2,1)}, bf16[256,4096]{1,0:T(8,128)(2,1)}, f32[8,48,512]{2,1,0:T(8,128)}, bf16[8,32,512]{2,1,0:T(8,128)(2,1)}) custom-call(s32[1]{0:T(128)} %bitcast.core, f32[8,16,512]{2,1,0:T(8,128)} %copy-done.1, f32[16,512]{1,0:T(8,128)} %residue.5, bf16[128,4096]{1,0:T(8,128)(2,1)} %get-tuple-element.36.x_keep, ...), custom_call_target="tpu_custom_call" | custom-call | flops 117440512 | bytes 8388608 | tf_op jit(solution)/shard_map/states/pallas_call | solution.py:281
  44.2 4.1 %all-to-all-start.1 = ((f32[8,48,512]{2,1,0:T(8,128)}), f32[8,48,512]{2,1,0:T(8,128)S(1)}, u32[]{:S(2)}, u32[]{:S(2)}) async-start(f32[8,48,512]{2,1,0:T(8,128)} %get-tuple-element.42), calls=%async_computation.1 | async-start | bytes 1572864 | tf_op jit(solution)/shard_map/all_to_all | solution.py:292
  48.3 0.7 collective-permute-start
  48.9 1.5 %collective-permute-done.prm_got = f32[8,16,512]{2,1,0:T(8,128)} collective-permute-done((f32[8,16,512]{2,1,0:T(8,128)}, f32[8,16,512]{2,1,0:T(8,128)}, u32[]{:S(2)}, u32[]{:S(2)}) %collective-permute-start) | collective-permute-done | bytes 262176 | tf_op jit(solution)/shard_map/ppermute | solution.py:287
  50.4 20.7 %local_grads.1.grad_b = bf16[8,32,512]{2,1,0:T(8,128)(2,1)} custom-call(f32[8,16,512]{2,1,0:T(8,128)} %copy-done.1, bf16[512,256]{1,0:T(8,128)(2,1)} %constant.23.clone.forward, bf16[256,512]{1,0:T(8,128)(2,1)} %constant.24.clone.inverse, bf16[256,4096]{1,0:T(8,128)(2,1)} %get-tuple-element.44.x, bf16[256,4096]{1,0:T(8,128)(2,1)} %get-tuple-element.45.g), custom_call_target="tpu_custom_call" | custom-call | flops 100663296 | bytes 4194304 | tf_op jit(solution)/shard_map/local_grads/pallas_call | solution.py:281
  71.1 0.0 all-to-all-done.1.sums.residue
  71.1 0.0 copy-start
  71.1 1.0 copy-done
  72.1 2.4 %scan.1 = bf16[8,128,512]{2,1,0:T(8,128)(2,1)} custom-call(f32[8,48,512]{2,1,0:T(8,128)} %copy-done, bf16[8,32,512]{2,1,0:T(8,128)(2,1)} %get-tuple-element.43.grad_a, bf16[8,32,512]{2,1,0:T(8,128)(2,1)} %local_grads.1.grad_b, f32[16,512]{1,0:T(8,128)} %own_rate.3, f32[16,512]{1,0:T(8,128)} %residue.5), custom_call_target="tpu_custom_call" | custom-call | tf_op jit(solution)/shard_map/scan/pallas_call | solution.py:348
  74.5 6.9 %all-to-all-start.2 = ((bf16[8,128,512]{2,1,0:T(8,128)(2,1)}), bf16[8,128,512]{2,1,0:T(8,128)(2,1)}, u32[]{:S(2)}, u32[]{:S(2)}) async-start(bf16[8,128,512]{2,1,0:T(8,128)(2,1)} %scan.1), calls=%async_computation.2 | async-start | bytes 2097152 | tf_op jit(solution)/shard_map/all_to_all | solution.py:292
  81.4 15.3 %local_conv.1 = (bf16[128,4096]{1,0:T(8,128)(2,1)}, bf16[128,4096]{1,0:T(8,128)(2,1)}, bf16[128,4096]{1,0:T(8,128)(2,1)}, bf16[128,4096]{1,0:T(8,128)(2,1)}) custom-call(s32[1]{0:T(128)} %bitcast.core, f32[8,16,512]{2,1,0:T(8,128)} %copy-done.1, f32[8,48,512]{2,1,0:T(8,128)} %copy-done, bf16[512,256]{1,0:T(8,128)(2,1)} %constant.23.clone.forward, ...), custom_call_target="tpu_custom_call" | custom-call | flops 83886080 | bytes 8388608 | tf_op jit(solution)/shard_map/local_conv/pallas_call | solution.py:281
  96.7 0.7 collective-permute-start.4
  97.4 0.1 collective-permute-start.5
  97.5 1.4 %all-to-all-done.2.got.ends = bf16[8,128,512]{2,1,0:T(8,128)(2,1)} async-done(((bf16[8,128,512]{2,1,0:T(8,128)(2,1)}), bf16[8,128,512]{2,1,0:T(8,128)(2,1)}, u32[]{:S(2)}, u32[]{:S(2)}) %all-to-all-start.2) | async-done | bytes 1048608 | tf_op jit(solution)/shard_map/all_to_all | solution.py:292
  98.9 0.8 collective-permute-start.3
  99.7 2.2 %owner_grads.1 = f32[8,32,512]{2,1,0:T(8,128)} custom-call(f32[8,48,512]{2,1,0:T(8,128)} %copy-done, bf16[8,128,512]{2,1,0:T(8,128)(2,1)} %all-to-all-done.2.got.ends, f32[16,512]{1,0:T(8,128)} %own_rate.3, f32[16,512]{1,0:T(8,128)} %residue.5), custom_call_target="tpu_custom_call" | custom-call | flops 1000 | bytes 2000000 | tf_op jit(solution)/shard_map/owner_grads/pallas_call | solution.py:281
  101.8 5.1 %all-to-all-start.3 = ((f32[8,32,512]{2,1,0:T(8,128)}), f32[8,32,512]{2,1,0:T(8,128)S(1)}, u32[]{:S(2)}, u32[]{:S(2)}) async-start(f32[8,32,512]{2,1,0:T(8,128)} %owner_grads.1), calls=%async_computation.3 | async-start | bytes 1048576 | tf_op jit(solution)/shard_map/all_to_all | solution.py:371
  107.0 0.0 collective-permute-done.4.conv_got
  107.0 0.0 collective-permute-done.5.back_got
  107.0 0.0 collective-permute-done.3.ends_got
  107.0 15.2 %finish.1 = (bf16[128,8192]{1,0:T(8,128)(2,1)}, bf16[128,8192]{1,0:T(8,128)(2,1)}, bf16[128,8192]{1,0:T(8,128)(2,1)}) custom-call(s32[1]{0:T(128)} %bitcast.core, f32[8,16,512]{2,1,0:T(8,128)} %copy-done.1, f32[8,16,512]{2,1,0:T(8,128)} %collective-permute-done.prm_got, bf16[8,128,512]{2,1,0:T(8,128)(2,1)} %all-to-all-done.2.got.ends, ...), custom_call_target="tpu_custom_call" | custom-call | flops 67108864 | bytes 20971520 | tf_op jit(solution)/shard_map/finish/pallas_call | solution.py:281
  122.2 0.0 all-to-all-done.3
  122.2 0.6 fusion
  (1 shorter events, 0.0 us)
Async XLA Ops:
  2.1 15.3 %all-to-all-start = ((f32[8,16,512]{2,1,0:T(8,128)}), f32[8,16,512]{2,1,0:T(8,128)S(1)}, u32[]{:S(2)}, u32[]{:S(2)}) async-start(f32[8,16,512]{2,1,0:T(8,128)} %rate_copies.1), calls=%async_computation | async-start | bytes 524288 | tf_op jit(solution)/shard_map/all_to_all | solution.py:292
  17.4 6.1 %copy-start.1 = (f32[8,16,512]{2,1,0:T(8,128)}, f32[8,16,512]{2,1,0:T(8,128)S(1)}, u32[]{:S(2)}) copy-start(f32[8,16,512]{2,1,0:T(8,128)S(1)} %all-to-all-done.prm) | copy-start | bytes 786436
  17.4 4.6 %collective-permute-start.1 = (bf16[128,4096]{1,0:T(8,128)(2,1)}, bf16[128,4096]{1,0:T(8,128)(2,1)}, u32[]{:S(2)}, u32[]{:S(2)}) collective-permute-start(bf16[128,4096]{1,0:T(8,128)(2,1)} %get-tuple-element.38), channel_id=1, source_target_pairs={{0,1},{1,0},{2,3},{3,2},{4,5},{5,4},{6,7},{7,6},{8,9},{9,8},{10,11... | collective-permute-start | bytes 3145736 | tf_op jit(solution)/shard_map/ppermute | solution.py:287
  19.3 4.1 %collective-permute-start.2 = (bf16[128,4096]{1,0:T(8,128)(2,1)}, bf16[128,4096]{1,0:T(8,128)(2,1)}, u32[]{:S(2)}, u32[]{:S(2)}) collective-permute-start(bf16[128,4096]{1,0:T(8,128)(2,1)} %get-tuple-element.39), channel_id=1, source_target_pairs={{0,1},{1,0},{2,3},{3,2},{4,5},{5,4},{6,7},{7,6},{8,9},{9,8},{10,11... | collective-permute-start | bytes 3145736 | tf_op jit(solution)/shard_map/ppermute | solution.py:287
  44.2 26.9 %all-to-all-start.1 = ((f32[8,48,512]{2,1,0:T(8,128)}), f32[8,48,512]{2,1,0:T(8,128)S(1)}, u32[]{:S(2)}, u32[]{:S(2)}) async-start(f32[8,48,512]{2,1,0:T(8,128)} %get-tuple-element.42), calls=%async_computation.1 | async-start | bytes 1572864 | tf_op jit(solution)/shard_map/all_to_all | solution.py:292
  48.3 2.2 %collective-permute-start = (f32[8,16,512]{2,1,0:T(8,128)}, f32[8,16,512]{2,1,0:T(8,128)}, u32[]{:S(2)}, u32[]{:S(2)}) collective-permute-start(f32[8,16,512]{2,1,0:T(8,128)} %copy-done.1), channel_id=1, source_target_pairs={{0,1},{1,0},{2,3},{3,2},{4,5},{5,4},{6,7},{7,6},{8,9},{9,8},{10,11... | collective-permute-start | bytes 786440 | tf_op jit(solution)/shard_map/ppermute | solution.py:287
  71.1 1.0 copy-start
  74.5 24.4 %all-to-all-start.2 = ((bf16[8,128,512]{2,1,0:T(8,128)(2,1)}), bf16[8,128,512]{2,1,0:T(8,128)(2,1)}, u32[]{:S(2)}, u32[]{:S(2)}) async-start(bf16[8,128,512]{2,1,0:T(8,128)(2,1)} %scan.1), calls=%async_computation.2 | async-start | bytes 2097152 | tf_op jit(solution)/shard_map/all_to_all | solution.py:292
  96.7 10.3 %collective-permute-start.4 = (bf16[128,4096]{1,0:T(8,128)(2,1)}, bf16[128,4096]{1,0:T(8,128)(2,1)}, u32[]{:S(2)}, u32[]{:S(2)}) collective-permute-start(bf16[128,4096]{1,0:T(8,128)(2,1)} %get-tuple-element.51), channel_id=1, source_target_pairs={{0,1},{1,0},{2,3},{3,2},{4,5},{5,4},{6,7},{7,6},{8,9},{9,8},{10,11... | collective-permute-start | bytes 3145736 | tf_op jit(solution)/shard_map/ppermute | solution.py:287
  97.4 9.6 %collective-permute-start.5 = (bf16[128,4096]{1,0:T(8,128)(2,1)}, bf16[128,4096]{1,0:T(8,128)(2,1)}, u32[]{:S(2)}, u32[]{:S(2)}) collective-permute-start(bf16[128,4096]{1,0:T(8,128)(2,1)} %get-tuple-element.52), channel_id=1, source_target_pairs={{0,1},{1,0},{2,3},{3,2},{4,5},{5,4},{6,7},{7,6},{8,9},{9,8},{10,11... | collective-permute-start | bytes 3145736 | tf_op jit(solution)/shard_map/ppermute | solution.py:287
  98.9 8.1 %collective-permute-start.3 = (bf16[8,128,512]{2,1,0:T(8,128)(2,1)}, bf16[8,128,512]{2,1,0:T(8,128)(2,1)}, u32[]{:S(2)}, u32[]{:S(2)}) collective-permute-start(bf16[8,128,512]{2,1,0:T(8,128)(2,1)} %all-to-all-done.2.got.ends), channel_id=1, source_target_pairs={{0,1},{1,0},{2,3},{3,2},{4,5},{5,4},{6,7},{7,6},{8,9},{9,8},{10,11... | collective-permute-start | bytes 3145736 | tf_op jit(solution)/shard_map/ppermute | solution.py:287
  101.8 20.3 %all-to-all-start.3 = ((f32[8,32,512]{2,1,0:T(8,128)}), f32[8,32,512]{2,1,0:T(8,128)S(1)}, u32[]{:S(2)}, u32[]{:S(2)}) async-start(f32[8,32,512]{2,1,0:T(8,128)} %owner_grads.1), calls=%async_computation.3 | async-start | bytes 1048576 | tf_op jit(solution)/shard_map/all_to_all | solution.py:371

commit v4 on v3

--- a/solution.py
+++ b/solution.py
@@ -28,7 +28,7 @@
     return forward.astype(ml_dtypes.bfloat16), inverse.astype(ml_dtypes.bfloat16)
 
 
-def params(vmem=63):
+def params(vmem=64):
     return pltpu.CompilerParams(vmem_limit_bytes=vmem * 1024 * 1024)
 
 
@@ -45,11 +45,6 @@
     while len(terms) > 1:
         terms = [u + v for u, v in zip(terms[::2], terms[1::2])]
     return terms[0]
-
-
-def copies_kernel(array, out):
-    for d in range(out.shape[0]):
-        out[d] = array[...]
 
 
 def gate_kernel(core, keys, values, out_grad, queries, x_keep, g_keep, x_give, g_give):
@@ -95,14 +90,9 @@
     return [[(vj, last * vj - dj) for vj, dj in zip(vi, di)] for vi, di in zip(v, d)]
 
 
-def state_kernel(core, prm, residue, x_keep, g_keep, x_got, g_got, x_out, g_out, sums, parts, x_s, g_s, sums_s):
-    low = pl.multiple_of(core[0] * HALF, HALF)
-    high = pl.multiple_of(HALF - core[0] * HALF, HALF)
-    for keep, got, out, wide in ((x_keep, x_got, x_out, x_s), (g_keep, g_got, g_out, g_s)):
-        for part, at in ((keep, low), (got, high)):
-            block = part[...]
-            out[pl.ds(at, HALF), :] = block
-            wide[pl.ds(at, HALF), :] = block.astype(F32)
+def state_kernel(prm, residue, x, g, sums, parts, x_s, g_s, sums_s):
+    x_s[...] = x[...].astype(F32)
+    g_s[...] = g[...].astype(F32)
     for tile in range(WIDTH // 128):
         lanes = pl.ds(128 * tile, 128)
         s, r = ladder(128), ladder(128, True)
@@ -142,11 +132,17 @@
     return dft(inverse, both)
 
 
-def grad_kernel(prm, forward, inverse, x, g, parts, lag_s, sums_s):
+def lag_kernel(core, forward, inverse, x_keep, g_keep, x_got, g_got, x_out, g_out, lag):
+    low = pl.multiple_of(core[0] * HALF, HALF)
+    high = pl.multiple_of(HALF - core[0] * HALF, HALF)
+    for keep, got, out in ((x_keep, x_got, x_out), (g_keep, g_got, g_out)):
+        out[pl.ds(low, HALF), :] = keep[...]
+        out[pl.ds(high, HALF), :] = got[...]
     fwd, inv = forward[...], inverse[...]
-    for part in range(WIDTH // PART):
-        lanes = pl.ds(PART * part, PART)
-        lag_s[:, lanes] = correlate(fwd, inv, dft(fwd, x[:, lanes]), dft(fwd, g[:, lanes]))
+    lag[...] = correlate(fwd, inv, dft(fwd, x_out[...]), dft(fwd, g_out[...]))
+
+
+def grad_kernel(prm, lag, grad_a, parts, sums_s):
     for tile in range(WIDTH // 128):
         lanes = pl.ds(128 * tile, 128)
         s = ladder(128)
@@ -154,7 +150,7 @@
         def some(group, carry):
             modes = [TOGETHER * group + i for i in range(TOGETHER)]
             rates = [prm[0, pl.ds(m, 1), lanes] for m in modes]
-            (lags,) = power_sums(rates, ((lag_s, False),), lanes)
+            (lags,) = power_sums(rates, ((lag, False),), lanes)
             for m, rate, (v, d) in zip(modes, rates, lags):
                 weight = jnp.exp(-rate * s)
                 sums_s[pl.ds(m, 1), lanes] = column(weight * v)
@@ -162,7 +158,8 @@
             return carry
 
         lax.fori_loop(0, MODES // TOGETHER, some, 0, unroll=True)
-    parts[0] = sums_s[...].astype(BF16)
+    parts[0, 0:32, :] = grad_a[0]
+    parts[0, 32:64, :] = sums_s[...].astype(BF16)
 
 
 def expand(minus, steps, heads, flip, put, count):
@@ -198,7 +195,7 @@
             give[:, lanes] = jnp.where(even, both[HALF:], both[:HALF])
 
 
-def scan_kernel(sums, grad_a, grad_b, own_rate, residue, out):
+def scan_kernel(sums, parts, own_rate, residue, out):
     rate = own_rate[...]
     scale = residue[...] * jnp.exp(-rate)
     far = jnp.exp(-float(LEN) * rate)
@@ -217,9 +214,6 @@
     for d in range(BLOCKS - 1, -1, -1):
         write(d, 2 * MODES, state)
         state = far * state + sums[d, MODES : 2 * MODES, :]
-    for d in range(BLOCKS):
-        out[d, 64:96, :] = grad_a[d]
-        out[d, 96:128, :] = grad_b[d]
 
 
 def owner_grad_kernel(sums, got, own_rate, residue, out):
@@ -274,12 +268,13 @@
         value_out[:, lanes] = product(b, keys[:, lanes])
 
 
-def call(kernel, name, work, grid, in_specs, out_specs, shapes, scratch, operands, prefetch=True):
+def call(kernel, name, work, grid, in_specs, out_specs, shapes, scratch, operands, prefetch=True, aliases=None):
     spec = pltpu.PrefetchScalarGridSpec(
         num_scalar_prefetch=1 if prefetch else 0, grid=grid, in_specs=in_specs, out_specs=out_specs, scratch_shapes=scratch
     )
     return pl.pallas_call(
-        kernel, grid_spec=spec, out_shape=shapes, compiler_params=params(), cost_estimate=work, name=name
+        kernel, grid_spec=spec, out_shape=shapes, compiler_params=params(), cost_estimate=work, name=name,
+        input_output_aliases=aliases or {},
     )(*operands)
 
 
@@ -297,15 +292,9 @@
     half = chans // 2
     queries2, keys2, values2, out_grad2 = (a.reshape(HALF, chans) for a in (queries, keys, values, out_grad))
     core = (lax.axis_index("ctx") % 2).astype(jnp.int32).reshape(1)
-    prm = exchange(
-        pl.pallas_call(
-            copies_kernel,
-            out_shape=jax.ShapeDtypeStruct((BLOCKS, MODES, WIDTH), F32),
-            compiler_params=params(),
-            name="rate_copies",
-        )(rate)
-    )
     forward, inverse = tables()
+    owned = lambda rows, i=0: pl.BlockSpec((BLOCKS, rows, WIDTH), lambda *_: (0, i, 0))
+    shape_payload = jax.ShapeDtypeStruct((BLOCKS, 128, WIDTH), BF16)
     work = LEN * half * MODES
     moved = LEN * half
 
@@ -331,26 +320,31 @@
         gate_kernel, "gate", cost(2 * moved, 12 * moved), (BLOCKS // 2,), [pair] * 4, [pair_half] * 4, [shape_part] * 4, [],
         (core, keys2, values2, out_grad2, queries2),
     )
-    x_give, g_give, prm = lax.optimization_barrier((x_give, g_give, prm))
-    x_got, g_got, prm_got = swap(x_give), swap(g_give), swap(prm)
-    x, g, sums, grad_a = call(
-        state_kernel, "states", cost(7 * work, 8 * moved), (BLOCKS,), [rows16, own] + [part] * 4,
-        [whole, whole, rows48, rows32],
-        [shape_whole, shape_whole, jax.ShapeDtypeStruct((BLOCKS, 48, WIDTH), F32), shape_rows],
-        [wide, wide, narrow], (core, prm, residue, x_keep, g_keep, x_got, g_got),
+    rates, x_give = lax.optimization_barrier((jnp.broadcast_to(rate[None], (BLOCKS, MODES, WIDTH)), x_give))
+    prm = exchange(rates)
+    x_got, g_got = swap(x_give), swap(g_give)
+    double = pl.BlockSpec((HALF, 2 * WIDTH), lambda q, *_: (0, q))
+    double_whole = pl.BlockSpec((LEN, 2 * WIDTH), lambda q, *_: (0, q))
+    x, g, lag = call(
+        lag_kernel, "lags", cost(work, 16 * moved), (BLOCKS // 2,), [table_f, table_i] + [double] * 4,
+        [double_whole] * 3, [shape_whole, shape_whole, jax.ShapeDtypeStruct((LEN, half), F32)], [],
+        (core, forward, inverse, x_keep, g_keep, x_got, g_got),
+    )
+    prm_got = swap(prm)
+    sums, grad_a = call(
+        state_kernel, "states", cost(7 * work, 4 * moved), (BLOCKS,), [rows16, own, whole, whole], [rows48, rows32],
+        [jax.ShapeDtypeStruct((BLOCKS, 48, WIDTH), F32), shape_rows], [wide, wide, narrow], (prm, residue, x, g), False,
     )
     sums_own = exchange(sums)
-    prm_got, x = lax.optimization_barrier((prm_got, x))
-    grad_b = call(
-        grad_kernel, "local_grads", cost(6 * work, 4 * moved), (BLOCKS,), [rows16, table_f, table_i, whole, whole],
-        rows32, shape_rows, [wide, narrow], (prm, forward, inverse, x, g), False,
-    )
-    ends_own = pl.pallas_call(
-        scan_kernel,
-        out_shape=jax.ShapeDtypeStruct((BLOCKS, 128, WIDTH), BF16),
-        compiler_params=params(),
-        name="scan",
-    )(sums_own, grad_a, grad_b, rate, residue)
+    parts = call(
+        grad_kernel, "local_grads", cost(4 * work, 4 * moved), (BLOCKS,), [rows16, whole, rows32],
+        pl.BlockSpec((1, 64, WIDTH), lambda q, *_: (q, 1, 0)), shape_payload, [narrow], (prm, lag, grad_a), False,
+    )
+    prm_got, parts = lax.optimization_barrier((prm_got, parts))
+    ends_own = call(
+        scan_kernel, "scan", cost(1000, 1000000), (1,), [owned(32), pl.BlockSpec(memory_space=pl.ANY), own, own], owned(64),
+        shape_payload, [], (sums_own, parts, rate, residue), False, {1: 0},
+    )
     ends = exchange(ends_own)
     few = pltpu.VMEM((MODES, WIDTH), F32)
     conv_keep, back_keep, conv_give, back_give = call(
@@ -361,7 +355,6 @@
     conv_got, back_got = swap(conv_give), swap(back_give)
     ends, conv_keep = lax.optimization_barrier((ends, conv_keep))
     ends_got = swap(ends)
-    owned = lambda rows, i=0: pl.BlockSpec((BLOCKS, rows, WIDTH), lambda *_: (0, i, 0))
     grads = call(
         owner_grad_kernel, "owner_grads", cost(1000, 2000000), (1,), [owned(32), owned(64, 1), own, own],
         pl.BlockSpec((8, 32, WIDTH), lambda *_: (0, 0, 0)), jax.ShapeDtypeStruct((8, 32, WIDTH), F32), [],

time: 124 us -> 116 us (0.935)
  waiting for transfers between devices: 8.98 us -> 2.9 us
  Pallas kernels: 83.7 us -> 80.5 us
    ppermute x6, waiting for transfers between devices: 5.64 us -> 0.02 us  [swap(): return lax.ppermute(array, 'ctx', [(i, i ^ 1) for i in range(2 * BLOCKS)])]
    pallas_call x2 -> x0, Pallas kernels: 3.87 us -> none  [the longest x1 2.39 us: body(): pl.pallas_call(scan_kernel, out_shape=jax.ShapeDtypeStruct((BLOCKS, 128,...]
    broadcast_in_dim x0 -> x1, local copies, waits for them, and re-layouts: none -> 1.48 us  [body(): jnp.broadcast_to(rate[None], (BLOCKS, MODES, WIDTH))]
    pallas_call x6 -> x8, Pallas kernels: 79.8 us -> 80.5 us  [call(): pl.pallas_call(kernel, grid_spec=spec, out_shape=shapes, compiler_params=...]
  transfers between devices with their start and end apart: 10 -> 10, of which waited for: 5 -> 2; matrix products, arithmetic and copies ran while one was open for 0% -> 0% of each run, Pallas kernels for 48% -> 45%
where the time goes in v4:
time: 116 us
  Pallas kernels  80.5 us (69%)
  starting transfers between devices  28.3 us (24%)
  waiting for transfers between devices  2.9 us (2%)
  local copies, waits for them, and re-layouts  2.11 us (2%)
    pallas_call x8, Pallas kernels, call(): pl.pallas_call(kernel, grid_spec=spec, out_shape=shapes, compiler_params=...  80.5 us
    all_to_all x3, starting transfers between devices, exchange(): lax.all_to_all(array, 'ctx', split_axis=0, concat_axis=0, axis_index_grou...  19.1 us
    all_to_all x1, starting transfers between devices, body(): grads = lax.all_to_all(grads, 'dp', split_axis=0, concat_axis=0, tiled=True)  5.15 us
    ppermute x6, starting transfers between devices, swap(): return lax.ppermute(array, 'ctx', [(i, i ^ 1) for i in range(2 * BLOCKS)])  4.08 us
    all_to_all x3, waiting for transfers between devices, exchange(): lax.all_to_all(array, 'ctx', split_axis=0, concat_axis=0, axis_index_grou...  2.88 us
  transfers between devices with their start and end apart: 10, of which 2 were waited for; matrix products, arithmetic and copies ran while one was open for 0% of the time, Pallas kernels for 45%

profile of v4, /device:TPU:1, one launch (start us, length us, event | category | flops | bytes accessed | tf_op | source)
XLA Modules:
  0.0 115.6 jit_solution(14955916947854056443)
XLA Ops:
  0.6 5.9 %gate.1 = (bf16[128,4096]{1,0:T(8,128)(2,1)}, bf16[128,4096]{1,0:T(8,128)(2,1)}, bf16[128,4096]{1,0:T(8,128)(2,1)}, bf16[128,4096]{1,0:T(8,128)(2,1)}) custom-call(s32[1]{0:T(128)} %bitcast.core, bf16[128,8192]{1,0:T(8,128)(2,1)} %bitcast.8, bf16[128,8192]{1,0:T(8,128)(2,1)} %bitcast.10, bf16[128,8192]{1,0:T(8,128)(2,1)} %bitcast.12, bf16[128,8192]{1,0:T(8,128)(2,1)} %bitcast.14), custom_call_target="tpu_custom_call" | custom-call | flops 2097152 | bytes 12582912 | tf_op jit(solution)/shard_map/gate/pallas_call | solution.py:275
  6.5 1.5 %broadcast_in_dim.2 = f32[8,16,512]{2,1,0:T(8,128)} broadcast(f32[16,512]{1,0:T(8,128)} %own_rate.3), dimensions={1,2} | broadcast | bytes 294912 | tf_op jit(solution)/shard_map/broadcast_in_dim | solution.py:323
  8.0 1.4 %collective-permute-start.1 = (bf16[128,4096]{1,0:T(8,128)(2,1)}, bf16[128,4096]{1,0:T(8,128)(2,1)}, u32[]{:S(2)}, u32[]{:S(2)}) collective-permute-start(bf16[128,4096]{1,0:T(8,128)(2,1)} %get-tuple-element.37), channel_id=1, source_target_pairs={{0,1},{1,0},{2,3},{3,2},{4,5},{5,4},{6,7},{7,6},{8,9},{9,8},{10,11... | collective-permute-start | bytes 3145736 | tf_op jit(solution)/shard_map/ppermute | solution.py:282
  9.4 0.0 collective-permute-start.2
  9.4 6.7 %all-to-all-start = ((f32[8,16,512]{2,1,0:T(8,128)}), f32[8,16,512]{2,1,0:T(8,128)}, u32[]{:S(2)}, u32[]{:S(2)}) async-start(f32[8,16,512]{2,1,0:T(8,128)} %broadcast_in_dim.2), calls=%async_computation | async-start | bytes 524288 | tf_op jit(solution)/shard_map/all_to_all | solution.py:287
  16.2 0.0 collective-permute-done.1.x_got
  16.2 0.0 collective-permute-done.2.g_got
  16.2 7.9 %lags.1 = (bf16[256,4096]{1,0:T(8,128)(2,1)}, bf16[256,4096]{1,0:T(8,128)(2,1)}, f32[256,4096]{1,0:T(8,128)}) custom-call(s32[1]{0:T(128)} %bitcast.core, bf16[512,256]{1,0:T(8,128)(2,1)} %constant.23.clone.forward, bf16[256,512]{1,0:T(8,128)(2,1)} %constant.24.clone.inverse, bf16[128,4096]{1,0:T(8,128)(2,1)} %get-tuple-element.35.x_keep, ...), custom_call_target="tpu_custom_call" | custom-call | flops 16777216 | bytes 16777216 | tf_op jit(solution)/shard_map/lags/pallas_call | solution.py:275
  24.1 0.0 all-to-all-done.prm
  24.1 20.1 %states.1 = (f32[8,48,512]{2,1,0:T(8,128)}, bf16[8,32,512]{2,1,0:T(8,128)(2,1)}) custom-call(f32[8,16,512]{2,1,0:T(8,128)} %all-to-all-done.prm, f32[16,512]{1,0:T(8,128)} %residue.5, bf16[256,4096]{1,0:T(8,128)(2,1)} %get-tuple-element.40.x, bf16[256,4096]{1,0:T(8,128)(2,1)} %get-tuple-element.41.g), custom_call_target="tpu_custom_call" | custom-call | flops 117440512 | bytes 4194304 | tf_op jit(solution)/shard_map/states/pallas_call | solution.py:275
  44.2 6.6 %all-to-all-start.1 = ((f32[8,48,512]{2,1,0:T(8,128)}), f32[8,48,512]{2,1,0:T(8,128)}, u32[]{:S(2)}, u32[]{:S(2)}) async-start(f32[8,48,512]{2,1,0:T(8,128)} %get-tuple-element.44), calls=%async_computation.1 | async-start | bytes 1572864 | tf_op jit(solution)/shard_map/all_to_all | solution.py:287
  50.8 1.3 %collective-permute-start = (f32[8,16,512]{2,1,0:T(8,128)}, f32[8,16,512]{2,1,0:T(8,128)}, u32[]{:S(2)}, u32[]{:S(2)}) collective-permute-start(f32[8,16,512]{2,1,0:T(8,128)} %all-to-all-done.prm), channel_id=1, source_target_pairs={{0,1},{1,0},{2,3},{3,2},{4,5},{5,4},{6,7},{7,6},{8,9},{9,8},{10,11... | collective-permute-start | bytes 786440 | tf_op jit(solution)/shard_map/ppermute | solution.py:282
  52.2 12.0 %local_grads.1.parts = bf16[8,128,512]{2,1,0:T(8,128)(2,1)} custom-call(f32[8,16,512]{2,1,0:T(8,128)} %all-to-all-done.prm, f32[256,4096]{1,0:T(8,128)} %get-tuple-element.39.lag, bf16[8,32,512]{2,1,0:T(8,128)(2,1)} %get-tuple-element.42.grad_a), custom_call_target="tpu_custom_call" | custom-call | flops 67108864 | bytes 4194304 | tf_op jit(solution)/shard_map/local_grads/pallas_call | solution.py:275
  64.2 0.0 collective-permute-done.prm_got
  64.2 1.2 %all-to-all-done.1.sums.residue = f32[8,48,512]{2,1,0:T(8,128)} async-done(((f32[8,48,512]{2,1,0:T(8,128)}), f32[8,48,512]{2,1,0:T(8,128)}, u32[]{:S(2)}, u32[]{:S(2)}) %all-to-all-start.1) | async-done | bytes 786464 | tf_op jit(solution)/shard_map/all_to_all | solution.py:287
  65.4 2.0 %scan.1 = bf16[8,128,512]{2,1,0:T(8,128)(2,1)} custom-call(f32[8,48,512]{2,1,0:T(8,128)} %all-to-all-done.1.sums.residue, bf16[8,128,512]{2,1,0:T(8,128)(2,1)} %local_grads.1.parts, f32[16,512]{1,0:T(8,128)} %own_rate.3, f32[16,512]{1,0:T(8,128)} %residue.5), custom_call_target="tpu_custom_call", output_to_operand_aliasing={{}: (1, {})} | custom-call | flops 1000 | bytes 1000000 | tf_op jit(solution)/shard_map/scan/pallas_call | solution.py:275
  67.4 5.7 %all-to-all-start.2 = ((bf16[8,128,512]{2,1,0:T(8,128)(2,1)}), bf16[8,128,512]{2,1,0:T(8,128)(2,1)}, u32[]{:S(2)}, u32[]{:S(2)}) async-start(bf16[8,128,512]{2,1,0:T(8,128)(2,1)} %scan.1), calls=%async_computation.2 | async-start | bytes 2097152 | tf_op jit(solution)/shard_map/all_to_all | solution.py:287
  73.1 15.3 %local_conv.1 = (bf16[128,4096]{1,0:T(8,128)(2,1)}, bf16[128,4096]{1,0:T(8,128)(2,1)}, bf16[128,4096]{1,0:T(8,128)(2,1)}, bf16[128,4096]{1,0:T(8,128)(2,1)}) custom-call(s32[1]{0:T(128)} %bitcast.core, f32[8,16,512]{2,1,0:T(8,128)} %all-to-all-done.prm, f32[8,48,512]{2,1,0:T(8,128)} %all-to-all-done.1.sums.residue, bf16[512,256]{1,0:T(8,128)(2,1)} %constant.23.clone.forward, ...), custom_call_target="tpu_custom_call" | custom-call | flops 83886080 | bytes 8388608 | tf_op jit(solution)/shard_map/local_conv/pallas_call | solution.py:275
  88.4 0.3 collective-permute-start.4
  88.7 0.2 collective-permute-start.5
  88.9 1.7 %all-to-all-done.2.got.ends = bf16[8,128,512]{2,1,0:T(8,128)(2,1)} async-done(((bf16[8,128,512]{2,1,0:T(8,128)(2,1)}), bf16[8,128,512]{2,1,0:T(8,128)(2,1)}, u32[]{:S(2)}, u32[]{:S(2)}) %all-to-all-start.2) | async-done | bytes 1048608 | tf_op jit(solution)/shard_map/all_to_all | solution.py:287
  90.6 0.8 collective-permute-start.3
  91.4 2.2 %owner_grads.1 = f32[8,32,512]{2,1,0:T(8,128)} custom-call(f32[8,48,512]{2,1,0:T(8,128)} %all-to-all-done.1.sums.residue, bf16[8,128,512]{2,1,0:T(8,128)(2,1)} %all-to-all-done.2.got.ends, f32[16,512]{1,0:T(8,128)} %own_rate.3, f32[16,512]{1,0:T(8,128)} %residue.5), custom_call_target="tpu_custom_call" | custom-call | flops 1000 | bytes 2000000 | tf_op jit(solution)/shard_map/owner_grads/pallas_call | solution.py:275
  93.5 5.1 %all-to-all-start.3 = ((f32[8,32,512]{2,1,0:T(8,128)}), f32[8,32,512]{2,1,0:T(8,128)}, u32[]{:S(2)}, u32[]{:S(2)}) async-start(f32[8,32,512]{2,1,0:T(8,128)} %owner_grads.1), calls=%async_computation.3 | async-start | bytes 1048576 | tf_op jit(solution)/shard_map/all_to_all | solution.py:364
  98.7 0.0 collective-permute-done.4.conv_got
  98.7 0.0 collective-permute-done.5.back_got
  98.7 0.0 collective-permute-done.3.ends_got
  98.7 15.2 %finish.1 = (bf16[128,8192]{1,0:T(8,128)(2,1)}, bf16[128,8192]{1,0:T(8,128)(2,1)}, bf16[128,8192]{1,0:T(8,128)(2,1)}) custom-call(s32[1]{0:T(128)} %bitcast.core, f32[8,16,512]{2,1,0:T(8,128)} %all-to-all-done.prm, f32[8,16,512]{2,1,0:T(8,128)} %collective-permute-done.prm_got, bf16[8,128,512]{2,1,0:T(8,128)(2,1)} %all-to-all-done.2.got.ends, ...), custom_call_target="tpu_custom_call" | custom-call | flops 67108864 | bytes 20971520 | tf_op jit(solution)/shard_map/finish/pallas_call | solution.py:275
  113.9 0.0 all-to-all-done.3
  113.9 1.1 reduce_sum.9
  115.0 0.6 fusion
Async XLA Ops:
  8.0 8.2 %collective-permute-start.1 = (bf16[128,4096]{1,0:T(8,128)(2,1)}, bf16[128,4096]{1,0:T(8,128)(2,1)}, u32[]{:S(2)}, u32[]{:S(2)}) collective-permute-start(bf16[128,4096]{1,0:T(8,128)(2,1)} %get-tuple-element.37), channel_id=1, source_target_pairs={{0,1},{1,0},{2,3},{3,2},{4,5},{5,4},{6,7},{7,6},{8,9},{9,8},{10,11... | collective-permute-start | bytes 3145736 | tf_op jit(solution)/shard_map/ppermute | solution.py:282
  9.4 6.7 %collective-permute-start.2 = (bf16[128,4096]{1,0:T(8,128)(2,1)}, bf16[128,4096]{1,0:T(8,128)(2,1)}, u32[]{:S(2)}, u32[]{:S(2)}) collective-permute-start(bf16[128,4096]{1,0:T(8,128)(2,1)} %get-tuple-element.38), channel_id=1, source_target_pairs={{0,1},{1,0},{2,3},{3,2},{4,5},{5,4},{6,7},{7,6},{8,9},{9,8},{10,11... | collective-permute-start | bytes 3145736 | tf_op jit(solution)/shard_map/ppermute | solution.py:282
  9.4 14.6 %all-to-all-start = ((f32[8,16,512]{2,1,0:T(8,128)}), f32[8,16,512]{2,1,0:T(8,128)}, u32[]{:S(2)}, u32[]{:S(2)}) async-start(f32[8,16,512]{2,1,0:T(8,128)} %broadcast_in_dim.2), calls=%async_computation | async-start | bytes 524288 | tf_op jit(solution)/shard_map/all_to_all | solution.py:287
  44.2 21.2 %all-to-all-start.1 = ((f32[8,48,512]{2,1,0:T(8,128)}), f32[8,48,512]{2,1,0:T(8,128)}, u32[]{:S(2)}, u32[]{:S(2)}) async-start(f32[8,48,512]{2,1,0:T(8,128)} %get-tuple-element.44), calls=%async_computation.1 | async-start | bytes 1572864 | tf_op jit(solution)/shard_map/all_to_all | solution.py:287
  50.8 13.4 %collective-permute-start = (f32[8,16,512]{2,1,0:T(8,128)}, f32[8,16,512]{2,1,0:T(8,128)}, u32[]{:S(2)}, u32[]{:S(2)}) collective-permute-start(f32[8,16,512]{2,1,0:T(8,128)} %all-to-all-done.prm), channel_id=1, source_target_pairs={{0,1},{1,0},{2,3},{3,2},{4,5},{5,4},{6,7},{7,6},{8,9},{9,8},{10,11... | collective-permute-start | bytes 786440 | tf_op jit(solution)/shard_map/ppermute | solution.py:282
  67.4 23.2 %all-to-all-start.2 = ((bf16[8,128,512]{2,1,0:T(8,128)(2,1)}), bf16[8,128,512]{2,1,0:T(8,128)(2,1)}, u32[]{:S(2)}, u32[]{:S(2)}) async-start(bf16[8,128,512]{2,1,0:T(8,128)(2,1)} %scan.1), calls=%async_computation.2 | async-start | bytes 2097152 | tf_op jit(solution)/shard_map/all_to_all | solution.py:287
  88.4 10.3 %collective-permute-start.4 = (bf16[128,4096]{1,0:T(8,128)(2,1)}, bf16[128,4096]{1,0:T(8,128)(2,1)}, u32[]{:S(2)}, u32[]{:S(2)}) collective-permute-start(bf16[128,4096]{1,0:T(8,128)(2,1)} %get-tuple-element.51), channel_id=1, source_target_pairs={{0,1},{1,0},{2,3},{3,2},{4,5},{5,4},{6,7},{7,6},{8,9},{9,8},{10,11... | collective-permute-start | bytes 3145736 | tf_op jit(solution)/shard_map/ppermute | solution.py:282
  88.7 10.0 %collective-permute-start.5 = (bf16[128,4096]{1,0:T(8,128)(2,1)}, bf16[128,4096]{1,0:T(8,128)(2,1)}, u32[]{:S(2)}, u32[]{:S(2)}) collective-permute-start(bf16[128,4096]{1,0:T(8,128)(2,1)} %get-tuple-element.52), channel_id=1, source_target_pairs={{0,1},{1,0},{2,3},{3,2},{4,5},{5,4},{6,7},{7,6},{8,9},{9,8},{10,11... | collective-permute-start | bytes 3145736 | tf_op jit(solution)/shard_map/ppermute | solution.py:282
  90.6 8.1 %collective-permute-start.3 = (bf16[8,128,512]{2,1,0:T(8,128)(2,1)}, bf16[8,128,512]{2,1,0:T(8,128)(2,1)}, u32[]{:S(2)}, u32[]{:S(2)}) collective-permute-start(bf16[8,128,512]{2,1,0:T(8,128)(2,1)} %all-to-all-done.2.got.ends), channel_id=1, source_target_pairs={{0,1},{1,0},{2,3},{3,2},{4,5},{5,4},{6,7},{7,6},{8,9},{9,8},{10,11... | collective-permute-start | bytes 3145736 | tf_op jit(solution)/shard_map/ppermute | solution.py:282
  93.5 20.3 %all-to-all-start.3 = ((f32[8,32,512]{2,1,0:T(8,128)}), f32[8,32,512]{2,1,0:T(8,128)}, u32[]{:S(2)}, u32[]{:S(2)}) async-start(f32[8,32,512]{2,1,0:T(8,128)} %owner_grads.1), calls=%async_computation.3 | async-start | bytes 1048576 | tf_op jit(solution)/shard_map/all_to_all | solution.py:364

commit v5 on v4

--- a/solution.py
+++ b/solution.py
@@ -47,8 +47,14 @@
     return terms[0]
 
 
-def gate_kernel(core, keys, values, out_grad, queries, x_keep, g_keep, x_give, g_give):
+def gate_kernel(core, rate, keys, values, out_grad, queries, copies, x_keep, g_keep, x_give, g_give):
     even = core[0] == 0
+
+    @pl.when(pl.program_id(0) == 0)
+    def _():
+        for q in range(BLOCKS):
+            copies[q] = rate[...]
+
     for left, right, keep, give in ((keys, values, x_keep, x_give), (out_grad, queries, g_keep, g_give)):
         for q in range(keep.shape[1] // WIDTH):
             first = pl.ds(2 * q * WIDTH, WIDTH)
@@ -238,6 +244,11 @@
         out[b, MODES : 2 * MODES, :] = second
 
 
+def sum_kernel(grads, residue_grad, rate_grad):
+    residue_grad[...] = total(grads[b, 0:MODES, :] for b in range(grads.shape[0]))
+    rate_grad[...] = total(grads[b, MODES : 2 * MODES, :] for b in range(grads.shape[0]))
+
+
 def finish_kernel(
     core, prm, prm_got, ends, ends_got, conv_keep, back_keep, conv_got, back_got, out_grad, keys, values,
     query_out, key_out, value_out, minus_s, step_s, head_s, tail_s, conv_s, back_s,
@@ -316,12 +327,13 @@
 
     pair = pl.BlockSpec((HALF, 4 * WIDTH), lambda q, *_: (0, q))
     pair_half = pl.BlockSpec((HALF, 2 * WIDTH), lambda q, *_: (0, q))
-    x_keep, g_keep, x_give, g_give = call(
-        gate_kernel, "gate", cost(2 * moved, 12 * moved), (BLOCKS // 2,), [pair] * 4, [pair_half] * 4, [shape_part] * 4, [],
-        (core, keys2, values2, out_grad2, queries2),
-    )
-    rates, x_give = lax.optimization_barrier((jnp.broadcast_to(rate[None], (BLOCKS, MODES, WIDTH)), x_give))
-    prm = exchange(rates)
+    copies, x_keep, g_keep, x_give, g_give = call(
+        gate_kernel, "gate", cost(2 * moved, 12 * moved), (BLOCKS // 2,), [own] + [pair] * 4,
+        [pl.BlockSpec((BLOCKS, MODES, WIDTH), lambda *_: (0, 0, 0))] + [pair_half] * 4,
+        [jax.ShapeDtypeStruct((BLOCKS, MODES, WIDTH), F32)] + [shape_part] * 4, [],
+        (core, rate, keys2, values2, out_grad2, queries2),
+    )
+    prm = exchange(copies)
     x_got, g_got = swap(x_give), swap(g_give)
     double = pl.BlockSpec((HALF, 2 * WIDTH), lambda q, *_: (0, q))
     double_whole = pl.BlockSpec((LEN, 2 * WIDTH), lambda q, *_: (0, q))
@@ -374,9 +386,14 @@
         (core, prm, prm_got, ends, ends_got, conv_keep, back_keep, conv_got, back_got, out_grad2, keys2, values2),
     )
     outs, grads = lax.optimization_barrier((outs, grads))
-    grads = jnp.sum(grads, 0)
+    residue_grad, rate_grad = pl.pallas_call(
+        sum_kernel,
+        out_shape=[jax.ShapeDtypeStruct((MODES, WIDTH), F32)] * 2,
+        compiler_params=params(),
+        name="sum_grads",
+    )(grads)
     query_grad, key_grad, value_grad = (a.reshape(queries.shape) for a in outs)
-    return query_grad, key_grad, value_grad, grads[:MODES], grads[MODES:]
+    return query_grad, key_grad, value_grad, residue_grad, rate_grad
 
 
 def solution(mesh):

time: 116 us -> 115 us (level)
  local copies, waits for them, and re-layouts: 2.11 us -> 0 us
  Pallas kernels: 80.5 us -> 82.2 us
    pallas_call x0 -> x1, Pallas kernels: none -> 1.69 us  [body(): pl.pallas_call(sum_kernel, out_shape=[jax.ShapeDtypeStruct((MODES, WIDTH)...]
    broadcast_in_dim x1 -> x0, local copies, waits for them, and re-layouts: 1.48 us -> none  [body(): jnp.broadcast_to(rate[None], (BLOCKS, MODES, WIDTH))]
  transfers between devices with their start and end apart: 10 -> 10, of which waited for: 2 -> 3; matrix products, arithmetic and copies ran while one was open for 0% -> 0% of each run, Pallas kernels for 45% -> 46%
where the time goes in v5:
time: 115 us; the launch traced here: 114 us
  Pallas kernels  82.2 us (71%)
  starting transfers between devices  28.1 us (24%)
  waiting for transfers between devices  3.21 us (3%)
    pallas_call x8, Pallas kernels, call(): pl.pallas_call(kernel, grid_spec=spec, out_shape=shapes, compiler_params=...  80.5 us
    all_to_all x3, starting transfers between devices, exchange(): lax.all_to_all(array, 'ctx', split_axis=0, concat_axis=0, axis_index_grou...  18.8 us
    all_to_all x1, starting transfers between devices, body(): grads = lax.all_to_all(grads, 'dp', split_axis=0, concat_axis=0, tiled=True)  5.15 us
    ppermute x6, starting transfers between devices, swap(): return lax.ppermute(array, 'ctx', [(i, i ^ 1) for i in range(2 * BLOCKS)])  4.1 us
    all_to_all x3, waiting for transfers between devices, exchange(): lax.all_to_all(array, 'ctx', split_axis=0, concat_axis=0, axis_index_grou...  3.19 us
  transfers between devices with their start and end apart: 10, of which 3 were waited for; matrix products, arithmetic and copies ran while one was open for 0% of the time, Pallas kernels for 46%

profile of v5, /device:TPU:1, one launch (start us, length us, event | category | flops | bytes accessed | tf_op | source)
XLA Modules:
  0.0 114.2 jit_solution(9550284007604248394)
XLA Ops:
  0.6 5.9 %gate.1 = (f32[8,16,512]{2,1,0:T(8,128)}, bf16[128,4096]{1,0:T(8,128)(2,1)}, bf16[128,4096]{1,0:T(8,128)(2,1)}, bf16[128,4096]{1,0:T(8,128)(2,1)}, bf16[128,4096]{1,0:T(8,128)(2,1)}) custom-call(s32[1]{0:T(128)} %bitcast.core, f32[16,512]{1,0:T(8,128)} %own_rate.3, bf16[128,8192]{1,0:T(8,128)(2,1)} %bitcast.8, bf16[128,8192]{1,0:T(8,128)(2,1)} %bitcast.10, ...), custom_call_target="tpu_custom_call" | custom-call | flops 2097152 | bytes 12582912 | tf_op jit(solution)/shard_map/gate/pallas_call | solution.py:286
  6.6 1.5 %collective-permute-start.1 = (bf16[128,4096]{1,0:T(8,128)(2,1)}, bf16[128,4096]{1,0:T(8,128)(2,1)}, u32[]{:S(2)}, u32[]{:S(2)}) collective-permute-start(bf16[128,4096]{1,0:T(8,128)(2,1)} %get-tuple-element.37), channel_id=1, source_target_pairs={{0,1},{1,0},{2,3},{3,2},{4,5},{5,4},{6,7},{7,6},{8,9},{9,8},{10,11... | collective-permute-start | bytes 3145736 | tf_op jit(solution)/shard_map/ppermute | solution.py:293
  8.0 0.1 collective-permute-start.2
  8.1 6.7 %all-to-all-start = ((f32[8,16,512]{2,1,0:T(8,128)}), f32[8,16,512]{2,1,0:T(8,128)}, u32[]{:S(2)}, u32[]{:S(2)}) async-start(f32[8,16,512]{2,1,0:T(8,128)} %get-tuple-element.34), calls=%async_computation | async-start | bytes 524288 | tf_op jit(solution)/shard_map/all_to_all | solution.py:298
  14.9 0.0 collective-permute-done.1.x_got
  14.9 0.0 collective-permute-done.2.g_got
  14.9 7.9 %lags.1 = (bf16[256,4096]{1,0:T(8,128)(2,1)}, bf16[256,4096]{1,0:T(8,128)(2,1)}, f32[256,4096]{1,0:T(8,128)}) custom-call(s32[1]{0:T(128)} %bitcast.core, bf16[512,256]{1,0:T(8,128)(2,1)} %constant.21.clone.forward, bf16[256,512]{1,0:T(8,128)(2,1)} %constant.22.clone.inverse, bf16[128,4096]{1,0:T(8,128)(2,1)} %get-tuple-element.35.x_keep, ...), custom_call_target="tpu_custom_call" | custom-call | flops 16777216 | bytes 16777216 | tf_op jit(solution)/shard_map/lags/pallas_call | solution.py:286
  22.8 0.2 all-to-all-done.prm
  23.0 20.1 %states.1 = (f32[8,48,512]{2,1,0:T(8,128)}, bf16[8,32,512]{2,1,0:T(8,128)(2,1)}) custom-call(f32[8,16,512]{2,1,0:T(8,128)} %all-to-all-done.prm, f32[16,512]{1,0:T(8,128)} %residue.5, bf16[256,4096]{1,0:T(8,128)(2,1)} %get-tuple-element.40.x, bf16[256,4096]{1,0:T(8,128)(2,1)} %get-tuple-element.41.g), custom_call_target="tpu_custom_call" | custom-call | flops 117440512 | bytes 4194304 | tf_op jit(solution)/shard_map/states/pallas_call | solution.py:286
  43.1 6.5 %all-to-all-start.1 = ((f32[8,48,512]{2,1,0:T(8,128)}), f32[8,48,512]{2,1,0:T(8,128)}, u32[]{:S(2)}, u32[]{:S(2)}) async-start(f32[8,48,512]{2,1,0:T(8,128)} %get-tuple-element.44), calls=%async_computation.1 | async-start | bytes 1572864 | tf_op jit(solution)/shard_map/all_to_all | solution.py:298
  49.5 1.2 %collective-permute-start = (f32[8,16,512]{2,1,0:T(8,128)}, f32[8,16,512]{2,1,0:T(8,128)}, u32[]{:S(2)}, u32[]{:S(2)}) collective-permute-start(f32[8,16,512]{2,1,0:T(8,128)} %all-to-all-done.prm), channel_id=1, source_target_pairs={{0,1},{1,0},{2,3},{3,2},{4,5},{5,4},{6,7},{7,6},{8,9},{9,8},{10,11... | collective-permute-start | bytes 786440 | tf_op jit(solution)/shard_map/ppermute | solution.py:293
  50.8 12.0 %local_grads.1.parts = bf16[8,128,512]{2,1,0:T(8,128)(2,1)} custom-call(f32[8,16,512]{2,1,0:T(8,128)} %all-to-all-done.prm, f32[256,4096]{1,0:T(8,128)} %get-tuple-element.39.lag, bf16[8,32,512]{2,1,0:T(8,128)(2,1)} %get-tuple-element.42.grad_a), custom_call_target="tpu_custom_call" | custom-call | flops 67108864 | bytes 4194304 | tf_op jit(solution)/shard_map/local_grads/pallas_call | solution.py:286
  62.8 0.0 collective-permute-done.prm_got
  62.8 1.3 %all-to-all-done.1.sums.residue = f32[8,48,512]{2,1,0:T(8,128)} async-done(((f32[8,48,512]{2,1,0:T(8,128)}), f32[8,48,512]{2,1,0:T(8,128)}, u32[]{:S(2)}, u32[]{:S(2)}) %all-to-all-start.1) | async-done | bytes 786464 | tf_op jit(solution)/shard_map/all_to_all | solution.py:298
  64.1 2.0 %scan.1 = bf16[8,128,512]{2,1,0:T(8,128)(2,1)} custom-call(f32[8,48,512]{2,1,0:T(8,128)} %all-to-all-done.1.sums.residue, bf16[8,128,512]{2,1,0:T(8,128)(2,1)} %local_grads.1.parts, f32[16,512]{1,0:T(8,128)} %own_rate.3, f32[16,512]{1,0:T(8,128)} %residue.5), custom_call_target="tpu_custom_call", output_to_operand_aliasing={{}: (1, {})} | custom-call | flops 1000 | bytes 1000000 | tf_op jit(solution)/shard_map/scan/pallas_call | solution.py:286
  66.1 5.6 %all-to-all-start.2 = ((bf16[8,128,512]{2,1,0:T(8,128)(2,1)}), bf16[8,128,512]{2,1,0:T(8,128)(2,1)}, u32[]{:S(2)}, u32[]{:S(2)}) async-start(bf16[8,128,512]{2,1,0:T(8,128)(2,1)} %scan.1), calls=%async_computation.2 | async-start | bytes 2097152 | tf_op jit(solution)/shard_map/all_to_all | solution.py:298
  71.7 15.3 %local_conv.1 = (bf16[128,4096]{1,0:T(8,128)(2,1)}, bf16[128,4096]{1,0:T(8,128)(2,1)}, bf16[128,4096]{1,0:T(8,128)(2,1)}, bf16[128,4096]{1,0:T(8,128)(2,1)}) custom-call(s32[1]{0:T(128)} %bitcast.core, f32[8,16,512]{2,1,0:T(8,128)} %all-to-all-done.prm, f32[8,48,512]{2,1,0:T(8,128)} %all-to-all-done.1.sums.residue, bf16[512,256]{1,0:T(8,128)(2,1)} %constant.21.clone.forward, ...), custom_call_target="tpu_custom_call" | custom-call | flops 83886080 | bytes 8388608 | tf_op jit(solution)/shard_map/local_conv/pallas_call | solution.py:286
  87.0 0.3 collective-permute-start.4
  87.3 0.2 collective-permute-start.5
  87.6 1.7 %all-to-all-done.2.got.ends = bf16[8,128,512]{2,1,0:T(8,128)(2,1)} async-done(((bf16[8,128,512]{2,1,0:T(8,128)(2,1)}), bf16[8,128,512]{2,1,0:T(8,128)(2,1)}, u32[]{:S(2)}, u32[]{:S(2)}) %all-to-all-start.2) | async-done | bytes 1048608 | tf_op jit(solution)/shard_map/all_to_all | solution.py:298
  89.2 0.8 collective-permute-start.3
  90.0 2.2 %owner_grads.1 = f32[8,32,512]{2,1,0:T(8,128)} custom-call(f32[8,48,512]{2,1,0:T(8,128)} %all-to-all-done.1.sums.residue, bf16[8,128,512]{2,1,0:T(8,128)(2,1)} %all-to-all-done.2.got.ends, f32[16,512]{1,0:T(8,128)} %own_rate.3, f32[16,512]{1,0:T(8,128)} %residue.5), custom_call_target="tpu_custom_call" | custom-call | flops 1000 | bytes 2000000 | tf_op jit(solution)/shard_map/owner_grads/pallas_call | solution.py:286
  92.1 5.2 %all-to-all-start.3 = ((f32[8,32,512]{2,1,0:T(8,128)}), f32[8,32,512]{2,1,0:T(8,128)}, u32[]{:S(2)}, u32[]{:S(2)}) async-start(f32[8,32,512]{2,1,0:T(8,128)} %owner_grads.1), calls=%async_computation.3 | async-start | bytes 1048576 | tf_op jit(solution)/shard_map/all_to_all | solution.py:376
  97.3 0.0 collective-permute-done.4.conv_got
  97.3 0.0 collective-permute-done.5.back_got
  97.3 0.0 collective-permute-done.3.ends_got
  97.3 15.2 %finish.1 = (bf16[128,8192]{1,0:T(8,128)(2,1)}, bf16[128,8192]{1,0:T(8,128)(2,1)}, bf16[128,8192]{1,0:T(8,128)(2,1)}) custom-call(s32[1]{0:T(128)} %bitcast.core, f32[8,16,512]{2,1,0:T(8,128)} %all-to-all-done.prm, f32[8,16,512]{2,1,0:T(8,128)} %collective-permute-done.prm_got, bf16[8,128,512]{2,1,0:T(8,128)(2,1)} %all-to-all-done.2.got.ends, ...), custom_call_target="tpu_custom_call" | custom-call | flops 67108864 | bytes 20971520 | tf_op jit(solution)/shard_map/finish/pallas_call | solution.py:286
  112.5 0.0 all-to-all-done.3.grads
  112.5 1.7 %sum_grads.1 = (f32[16,512]{1,0:T(8,128)}, f32[16,512]{1,0:T(8,128)}) custom-call(f32[8,32,512]{2,1,0:T(8,128)} %all-to-all-done.3.grads), custom_call_target="tpu_custom_call" | custom-call | tf_op jit(solution)/shard_map/sum_grads/pallas_call | solution.py:389
Async XLA Ops:
  6.6 8.3 %collective-permute-start.1 = (bf16[128,4096]{1,0:T(8,128)(2,1)}, bf16[128,4096]{1,0:T(8,128)(2,1)}, u32[]{:S(2)}, u32[]{:S(2)}) collective-permute-start(bf16[128,4096]{1,0:T(8,128)(2,1)} %get-tuple-element.37), channel_id=1, source_target_pairs={{0,1},{1,0},{2,3},{3,2},{4,5},{5,4},{6,7},{7,6},{8,9},{9,8},{10,11... | collective-permute-start | bytes 3145736 | tf_op jit(solution)/shard_map/ppermute | solution.py:293
  8.0 6.8 %collective-permute-start.2 = (bf16[128,4096]{1,0:T(8,128)(2,1)}, bf16[128,4096]{1,0:T(8,128)(2,1)}, u32[]{:S(2)}, u32[]{:S(2)}) collective-permute-start(bf16[128,4096]{1,0:T(8,128)(2,1)} %get-tuple-element.38), channel_id=1, source_target_pairs={{0,1},{1,0},{2,3},{3,2},{4,5},{5,4},{6,7},{7,6},{8,9},{9,8},{10,11... | collective-permute-start | bytes 3145736 | tf_op jit(solution)/shard_map/ppermute | solution.py:293
  8.1 14.9 %all-to-all-start = ((f32[8,16,512]{2,1,0:T(8,128)}), f32[8,16,512]{2,1,0:T(8,128)}, u32[]{:S(2)}, u32[]{:S(2)}) async-start(f32[8,16,512]{2,1,0:T(8,128)} %get-tuple-element.34), calls=%async_computation | async-start | bytes 524288 | tf_op jit(solution)/shard_map/all_to_all | solution.py:298
  43.1 21.1 %all-to-all-start.1 = ((f32[8,48,512]{2,1,0:T(8,128)}), f32[8,48,512]{2,1,0:T(8,128)}, u32[]{:S(2)}, u32[]{:S(2)}) async-start(f32[8,48,512]{2,1,0:T(8,128)} %get-tuple-element.44), calls=%async_computation.1 | async-start | bytes 1572864 | tf_op jit(solution)/shard_map/all_to_all | solution.py:298
  49.5 13.3 %collective-permute-start = (f32[8,16,512]{2,1,0:T(8,128)}, f32[8,16,512]{2,1,0:T(8,128)}, u32[]{:S(2)}, u32[]{:S(2)}) collective-permute-start(f32[8,16,512]{2,1,0:T(8,128)} %all-to-all-done.prm), channel_id=1, source_target_pairs={{0,1},{1,0},{2,3},{3,2},{4,5},{5,4},{6,7},{7,6},{8,9},{9,8},{10,11... | collective-permute-start | bytes 786440 | tf_op jit(solution)/shard_map/ppermute | solution.py:293
  66.1 23.1 %all-to-all-start.2 = ((bf16[8,128,512]{2,1,0:T(8,128)(2,1)}), bf16[8,128,512]{2,1,0:T(8,128)(2,1)}, u32[]{:S(2)}, u32[]{:S(2)}) async-start(bf16[8,128,512]{2,1,0:T(8,128)(2,1)} %scan.1), calls=%async_computation.2 | async-start | bytes 2097152 | tf_op jit(solution)/shard_map/all_to_all | solution.py:298
  87.0 10.3 %collective-permute-start.4 = (bf16[128,4096]{1,0:T(8,128)(2,1)}, bf16[128,4096]{1,0:T(8,128)(2,1)}, u32[]{:S(2)}, u32[]{:S(2)}) collective-permute-start(bf16[128,4096]{1,0:T(8,128)(2,1)} %get-tuple-element.51), channel_id=1, source_target_pairs={{0,1},{1,0},{2,3},{3,2},{4,5},{5,4},{6,7},{7,6},{8,9},{9,8},{10,11... | collective-permute-start | bytes 3145736 | tf_op jit(solution)/shard_map/ppermute | solution.py:293
  87.3 10.0 %collective-permute-start.5 = (bf16[128,4096]{1,0:T(8,128)(2,1)}, bf16[128,4096]{1,0:T(8,128)(2,1)}, u32[]{:S(2)}, u32[]{:S(2)}) collective-permute-start(bf16[128,4096]{1,0:T(8,128)(2,1)} %get-tuple-element.52), channel_id=1, source_target_pairs={{0,1},{1,0},{2,3},{3,2},{4,5},{5,4},{6,7},{7,6},{8,9},{9,8},{10,11... | collective-permute-start | bytes 3145736 | tf_op jit(solution)/shard_map/ppermute | solution.py:293
  89.2 8.1 %collective-permute-start.3 = (bf16[8,128,512]{2,1,0:T(8,128)(2,1)}, bf16[8,128,512]{2,1,0:T(8,128)(2,1)}, u32[]{:S(2)}, u32[]{:S(2)}) collective-permute-start(bf16[8,128,512]{2,1,0:T(8,128)(2,1)} %all-to-all-done.2.got.ends), channel_id=1, source_target_pairs={{0,1},{1,0},{2,3},{3,2},{4,5},{5,4},{6,7},{7,6},{8,9},{9,8},{10,11... | collective-permute-start | bytes 3145736 | tf_op jit(solution)/shard_map/ppermute | solution.py:293
  92.1 20.3 %all-to-all-start.3 = ((f32[8,32,512]{2,1,0:T(8,128)}), f32[8,32,512]{2,1,0:T(8,128)}, u32[]{:S(2)}, u32[]{:S(2)}) async-start(f32[8,32,512]{2,1,0:T(8,128)} %owner_grads.1), calls=%async_computation.3 | async-start | bytes 1048576 | tf_op jit(solution)/shard_map/all_to_all | solution.py:376

commit v6 on v5

--- a/solution.py
+++ b/solution.py
@@ -325,10 +325,10 @@
     wide = pltpu.VMEM((LEN, WIDTH), F32)
     narrow = pltpu.VMEM((32, WIDTH), F32)
 
-    pair = pl.BlockSpec((HALF, 4 * WIDTH), lambda q, *_: (0, q))
-    pair_half = pl.BlockSpec((HALF, 2 * WIDTH), lambda q, *_: (0, q))
+    pair = pl.BlockSpec((HALF, 8 * WIDTH), lambda q, *_: (0, q))
+    pair_half = pl.BlockSpec((HALF, 4 * WIDTH), lambda q, *_: (0, q))
     copies, x_keep, g_keep, x_give, g_give = call(
-        gate_kernel, "gate", cost(2 * moved, 12 * moved), (BLOCKS // 2,), [own] + [pair] * 4,
+        gate_kernel, "gate", cost(2 * moved, 12 * moved), (BLOCKS // 4,), [own] + [pair] * 4,
         [pl.BlockSpec((BLOCKS, MODES, WIDTH), lambda *_: (0, 0, 0))] + [pair_half] * 4,
         [jax.ShapeDtypeStruct((BLOCKS, MODES, WIDTH), F32)] + [shape_part] * 4, [],
         (core, rate, keys2, values2, out_grad2, queries2),

time: 115 us -> 114 us (level)
  no operation moved by 1% of the time
where the time goes in v6:
time: 114 us; the launch traced here: 113 us
  Pallas kernels  81.5 us (71%)
  starting transfers between devices  28.1 us (25%)
  waiting for transfers between devices  3.19 us (3%)
    pallas_call x8, Pallas kernels, call(): pl.pallas_call(kernel, grid_spec=spec, out_shape=shapes, compiler_params=...  79.8 us
    all_to_all x3, starting transfers between devices, exchange(): lax.all_to_all(array, 'ctx', split_axis=0, concat_axis=0, axis_index_grou...  18.8 us
    all_to_all x1, starting transfers between devices, body(): grads = lax.all_to_all(grads, 'dp', split_axis=0, concat_axis=0, tiled=True)  5.15 us
    ppermute x6, starting transfers between devices, swap(): return lax.ppermute(array, 'ctx', [(i, i ^ 1) for i in range(2 * BLOCKS)])  4.07 us
    all_to_all x3, waiting for transfers between devices, exchange(): lax.all_to_all(array, 'ctx', split_axis=0, concat_axis=0, axis_index_grou...  3.17 us
  transfers between devices with their start and end apart: 10, of which 3 were waited for; matrix products, arithmetic and copies ran while one was open for 0% of the time, Pallas kernels for 46%

profile of v6, /device:TPU:1, one launch (start us, length us, event | category | flops | bytes accessed | tf_op | source)
XLA Modules:
  0.0 113.4 jit_solution(15508691096438773420)
XLA Ops:
  0.6 5.2 %gate.1 = (f32[8,16,512]{2,1,0:T(8,128)}, bf16[128,4096]{1,0:T(8,128)(2,1)}, bf16[128,4096]{1,0:T(8,128)(2,1)}, bf16[128,4096]{1,0:T(8,128)(2,1)}, bf16[128,4096]{1,0:T(8,128)(2,1)}) custom-call(s32[1]{0:T(128)} %bitcast.core, f32[16,512]{1,0:T(8,128)} %own_rate.3, bf16[128,8192]{1,0:T(8,128)(2,1)} %bitcast.8, bf16[128,8192]{1,0:T(8,128)(2,1)} %bitcast.10, ...), custom_call_target="tpu_custom_call" | custom-call | flops 2097152 | bytes 12582912 | tf_op jit(solution)/shard_map/gate/pallas_call | solution.py:286
  5.8 1.4 %collective-permute-start.1 = (bf16[128,4096]{1,0:T(8,128)(2,1)}, bf16[128,4096]{1,0:T(8,128)(2,1)}, u32[]{:S(2)}, u32[]{:S(2)}) collective-permute-start(bf16[128,4096]{1,0:T(8,128)(2,1)} %get-tuple-element.37), channel_id=1, source_target_pairs={{0,1},{1,0},{2,3},{3,2},{4,5},{5,4},{6,7},{7,6},{8,9},{9,8},{10,11... | collective-permute-start | bytes 3145736 | tf_op jit(solution)/shard_map/ppermute | solution.py:293
  7.2 0.1 collective-permute-start.2
  7.3 6.7 %all-to-all-start = ((f32[8,16,512]{2,1,0:T(8,128)}), f32[8,16,512]{2,1,0:T(8,128)}, u32[]{:S(2)}, u32[]{:S(2)}) async-start(f32[8,16,512]{2,1,0:T(8,128)} %get-tuple-element.34), calls=%async_computation | async-start | bytes 524288 | tf_op jit(solution)/shard_map/all_to_all | solution.py:298
  14.1 0.0 collective-permute-done.1.x_got
  14.1 0.0 collective-permute-done.2.g_got
  14.1 7.9 %lags.1 = (bf16[256,4096]{1,0:T(8,128)(2,1)}, bf16[256,4096]{1,0:T(8,128)(2,1)}, f32[256,4096]{1,0:T(8,128)}) custom-call(s32[1]{0:T(128)} %bitcast.core, bf16[512,256]{1,0:T(8,128)(2,1)} %constant.21.clone.forward, bf16[256,512]{1,0:T(8,128)(2,1)} %constant.22.clone.inverse, bf16[128,4096]{1,0:T(8,128)(2,1)} %get-tuple-element.35.x_keep, ...), custom_call_target="tpu_custom_call" | custom-call | flops 16777216 | bytes 16777216 | tf_op jit(solution)/shard_map/lags/pallas_call | solution.py:286
  22.0 0.2 all-to-all-done.prm
  22.2 20.1 %states.1 = (f32[8,48,512]{2,1,0:T(8,128)}, bf16[8,32,512]{2,1,0:T(8,128)(2,1)}) custom-call(f32[8,16,512]{2,1,0:T(8,128)} %all-to-all-done.prm, f32[16,512]{1,0:T(8,128)} %residue.5, bf16[256,4096]{1,0:T(8,128)(2,1)} %get-tuple-element.40.x, bf16[256,4096]{1,0:T(8,128)(2,1)} %get-tuple-element.41.g), custom_call_target="tpu_custom_call" | custom-call | flops 117440512 | bytes 4194304 | tf_op jit(solution)/shard_map/states/pallas_call | solution.py:286
  42.3 6.5 %all-to-all-start.1 = ((f32[8,48,512]{2,1,0:T(8,128)}), f32[8,48,512]{2,1,0:T(8,128)}, u32[]{:S(2)}, u32[]{:S(2)}) async-start(f32[8,48,512]{2,1,0:T(8,128)} %get-tuple-element.44), calls=%async_computation.1 | async-start | bytes 1572864 | tf_op jit(solution)/shard_map/all_to_all | solution.py:298
  48.7 1.3 %collective-permute-start = (f32[8,16,512]{2,1,0:T(8,128)}, f32[8,16,512]{2,1,0:T(8,128)}, u32[]{:S(2)}, u32[]{:S(2)}) collective-permute-start(f32[8,16,512]{2,1,0:T(8,128)} %all-to-all-done.prm), channel_id=1, source_target_pairs={{0,1},{1,0},{2,3},{3,2},{4,5},{5,4},{6,7},{7,6},{8,9},{9,8},{10,11... | collective-permute-start | bytes 786440 | tf_op jit(solution)/shard_map/ppermute | solution.py:293
  50.0 12.0 %local_grads.1.parts = bf16[8,128,512]{2,1,0:T(8,128)(2,1)} custom-call(f32[8,16,512]{2,1,0:T(8,128)} %all-to-all-done.prm, f32[256,4096]{1,0:T(8,128)} %get-tuple-element.39.lag, bf16[8,32,512]{2,1,0:T(8,128)(2,1)} %get-tuple-element.42.grad_a), custom_call_target="tpu_custom_call" | custom-call | flops 67108864 | bytes 4194304 | tf_op jit(solution)/shard_map/local_grads/pallas_call | solution.py:286
  62.0 0.0 collective-permute-done.prm_got
  62.0 1.3 %all-to-all-done.1.sums.residue = f32[8,48,512]{2,1,0:T(8,128)} async-done(((f32[8,48,512]{2,1,0:T(8,128)}), f32[8,48,512]{2,1,0:T(8,128)}, u32[]{:S(2)}, u32[]{:S(2)}) %all-to-all-start.1) | async-done | bytes 786464 | tf_op jit(solution)/shard_map/all_to_all | solution.py:298
  63.3 2.0 %scan.1 = bf16[8,128,512]{2,1,0:T(8,128)(2,1)} custom-call(f32[8,48,512]{2,1,0:T(8,128)} %all-to-all-done.1.sums.residue, bf16[8,128,512]{2,1,0:T(8,128)(2,1)} %local_grads.1.parts, f32[16,512]{1,0:T(8,128)} %own_rate.3, f32[16,512]{1,0:T(8,128)} %residue.5), custom_call_target="tpu_custom_call", output_to_operand_aliasing={{}: (1, {})} | custom-call | flops 1000 | bytes 1000000 | tf_op jit(solution)/shard_map/scan/pallas_call | solution.py:286
  65.3 5.6 %all-to-all-start.2 = ((bf16[8,128,512]{2,1,0:T(8,128)(2,1)}), bf16[8,128,512]{2,1,0:T(8,128)(2,1)}, u32[]{:S(2)}, u32[]{:S(2)}) async-start(bf16[8,128,512]{2,1,0:T(8,128)(2,1)} %scan.1), calls=%async_computation.2 | async-start | bytes 2097152 | tf_op jit(solution)/shard_map/all_to_all | solution.py:298
  70.9 15.3 %local_conv.1 = (bf16[128,4096]{1,0:T(8,128)(2,1)}, bf16[128,4096]{1,0:T(8,128)(2,1)}, bf16[128,4096]{1,0:T(8,128)(2,1)}, bf16[128,4096]{1,0:T(8,128)(2,1)}) custom-call(s32[1]{0:T(128)} %bitcast.core, f32[8,16,512]{2,1,0:T(8,128)} %all-to-all-done.prm, f32[8,48,512]{2,1,0:T(8,128)} %all-to-all-done.1.sums.residue, bf16[512,256]{1,0:T(8,128)(2,1)} %constant.21.clone.forward, ...), custom_call_target="tpu_custom_call" | custom-call | flops 83886080 | bytes 8388608 | tf_op jit(solution)/shard_map/local_conv/pallas_call | solution.py:286
  86.2 0.3 collective-permute-start.4
  86.5 0.2 collective-permute-start.5
  86.8 1.7 %all-to-all-done.2.got.ends = bf16[8,128,512]{2,1,0:T(8,128)(2,1)} async-done(((bf16[8,128,512]{2,1,0:T(8,128)(2,1)}), bf16[8,128,512]{2,1,0:T(8,128)(2,1)}, u32[]{:S(2)}, u32[]{:S(2)}) %all-to-all-start.2) | async-done | bytes 1048608 | tf_op jit(solution)/shard_map/all_to_all | solution.py:298
  88.4 0.8 collective-permute-start.3
  89.2 2.2 %owner_grads.1 = f32[8,32,512]{2,1,0:T(8,128)} custom-call(f32[8,48,512]{2,1,0:T(8,128)} %all-to-all-done.1.sums.residue, bf16[8,128,512]{2,1,0:T(8,128)(2,1)} %all-to-all-done.2.got.ends, f32[16,512]{1,0:T(8,128)} %own_rate.3, f32[16,512]{1,0:T(8,128)} %residue.5), custom_call_target="tpu_custom_call" | custom-call | flops 1000 | bytes 2000000 | tf_op jit(solution)/shard_map/owner_grads/pallas_call | solution.py:286
  91.3 5.2 %all-to-all-start.3 = ((f32[8,32,512]{2,1,0:T(8,128)}), f32[8,32,512]{2,1,0:T(8,128)}, u32[]{:S(2)}, u32[]{:S(2)}) async-start(f32[8,32,512]{2,1,0:T(8,128)} %owner_grads.1), calls=%async_computation.3 | async-start | bytes 1048576 | tf_op jit(solution)/shard_map/all_to_all | solution.py:376
  96.5 0.0 collective-permute-done.4.conv_got
  96.5 0.0 collective-permute-done.5.back_got
  96.5 0.0 collective-permute-done.3.ends_got
  96.5 15.2 %finish.1 = (bf16[128,8192]{1,0:T(8,128)(2,1)}, bf16[128,8192]{1,0:T(8,128)(2,1)}, bf16[128,8192]{1,0:T(8,128)(2,1)}) custom-call(s32[1]{0:T(128)} %bitcast.core, f32[8,16,512]{2,1,0:T(8,128)} %all-to-all-done.prm, f32[8,16,512]{2,1,0:T(8,128)} %collective-permute-done.prm_got, bf16[8,128,512]{2,1,0:T(8,128)(2,1)} %all-to-all-done.2.got.ends, ...), custom_call_target="tpu_custom_call" | custom-call | flops 67108864 | bytes 20971520 | tf_op jit(solution)/shard_map/finish/pallas_call | solution.py:286
  111.7 0.0 all-to-all-done.3.grads
  111.7 1.7 %sum_grads.1 = (f32[16,512]{1,0:T(8,128)}, f32[16,512]{1,0:T(8,128)}) custom-call(f32[8,32,512]{2,1,0:T(8,128)} %all-to-all-done.3.grads), custom_call_target="tpu_custom_call" | custom-call | tf_op jit(solution)/shard_map/sum_grads/pallas_call | solution.py:389
Async XLA Ops:
  5.8 8.2 %collective-permute-start.1 = (bf16[128,4096]{1,0:T(8,128)(2,1)}, bf16[128,4096]{1,0:T(8,128)(2,1)}, u32[]{:S(2)}, u32[]{:S(2)}) collective-permute-start(bf16[128,4096]{1,0:T(8,128)(2,1)} %get-tuple-element.37), channel_id=1, source_target_pairs={{0,1},{1,0},{2,3},{3,2},{4,5},{5,4},{6,7},{7,6},{8,9},{9,8},{10,11... | collective-permute-start | bytes 3145736 | tf_op jit(solution)/shard_map/ppermute | solution.py:293
  7.2 6.8 %collective-permute-start.2 = (bf16[128,4096]{1,0:T(8,128)(2,1)}, bf16[128,4096]{1,0:T(8,128)(2,1)}, u32[]{:S(2)}, u32[]{:S(2)}) collective-permute-start(bf16[128,4096]{1,0:T(8,128)(2,1)} %get-tuple-element.38), channel_id=1, source_target_pairs={{0,1},{1,0},{2,3},{3,2},{4,5},{5,4},{6,7},{7,6},{8,9},{9,8},{10,11... | collective-permute-start | bytes 3145736 | tf_op jit(solution)/shard_map/ppermute | solution.py:293
  7.3 14.8 %all-to-all-start = ((f32[8,16,512]{2,1,0:T(8,128)}), f32[8,16,512]{2,1,0:T(8,128)}, u32[]{:S(2)}, u32[]{:S(2)}) async-start(f32[8,16,512]{2,1,0:T(8,128)} %get-tuple-element.34), calls=%async_computation | async-start | bytes 524288 | tf_op jit(solution)/shard_map/all_to_all | solution.py:298
  42.3 21.1 %all-to-all-start.1 = ((f32[8,48,512]{2,1,0:T(8,128)}), f32[8,48,512]{2,1,0:T(8,128)}, u32[]{:S(2)}, u32[]{:S(2)}) async-start(f32[8,48,512]{2,1,0:T(8,128)} %get-tuple-element.44), calls=%async_computation.1 | async-start | bytes 1572864 | tf_op jit(solution)/shard_map/all_to_all | solution.py:298
  48.7 13.3 %collective-permute-start = (f32[8,16,512]{2,1,0:T(8,128)}, f32[8,16,512]{2,1,0:T(8,128)}, u32[]{:S(2)}, u32[]{:S(2)}) collective-permute-start(f32[8,16,512]{2,1,0:T(8,128)} %all-to-all-done.prm), channel_id=1, source_target_pairs={{0,1},{1,0},{2,3},{3,2},{4,5},{5,4},{6,7},{7,6},{8,9},{9,8},{10,11... | collective-permute-start | bytes 786440 | tf_op jit(solution)/shard_map/ppermute | solution.py:293
  65.3 23.1 %all-to-all-start.2 = ((bf16[8,128,512]{2,1,0:T(8,128)(2,1)}), bf16[8,128,512]{2,1,0:T(8,128)(2,1)}, u32[]{:S(2)}, u32[]{:S(2)}) async-start(bf16[8,128,512]{2,1,0:T(8,128)(2,1)} %scan.1), calls=%async_computation.2 | async-start | bytes 2097152 | tf_op jit(solution)/shard_map/all_to_all | solution.py:298
  86.2 10.3 %collective-permute-start.4 = (bf16[128,4096]{1,0:T(8,128)(2,1)}, bf16[128,4096]{1,0:T(8,128)(2,1)}, u32[]{:S(2)}, u32[]{:S(2)}) collective-permute-start(bf16[128,4096]{1,0:T(8,128)(2,1)} %get-tuple-element.51), channel_id=1, source_target_pairs={{0,1},{1,0},{2,3},{3,2},{4,5},{5,4},{6,7},{7,6},{8,9},{9,8},{10,11... | collective-permute-start | bytes 3145736 | tf_op jit(solution)/shard_map/ppermute | solution.py:293
  86.5 10.0 %collective-permute-start.5 = (bf16[128,4096]{1,0:T(8,128)(2,1)}, bf16[128,4096]{1,0:T(8,128)(2,1)}, u32[]{:S(2)}, u32[]{:S(2)}) collective-permute-start(bf16[128,4096]{1,0:T(8,128)(2,1)} %get-tuple-element.52), channel_id=1, source_target_pairs={{0,1},{1,0},{2,3},{3,2},{4,5},{5,4},{6,7},{7,6},{8,9},{9,8},{10,11... | collective-permute-start | bytes 3145736 | tf_op jit(solution)/shard_map/ppermute | solution.py:293
  88.4 8.1 %collective-permute-start.3 = (bf16[8,128,512]{2,1,0:T(8,128)(2,1)}, bf16[8,128,512]{2,1,0:T(8,128)(2,1)}, u32[]{:S(2)}, u32[]{:S(2)}) collective-permute-start(bf16[8,128,512]{2,1,0:T(8,128)(2,1)} %all-to-all-done.2.got.ends), channel_id=1, source_target_pairs={{0,1},{1,0},{2,3},{3,2},{4,5},{5,4},{6,7},{7,6},{8,9},{9,8},{10,11... | collective-permute-start | bytes 3145736 | tf_op jit(solution)/shard_map/ppermute | solution.py:293
  91.3 20.3 %all-to-all-start.3 = ((f32[8,32,512]{2,1,0:T(8,128)}), f32[8,32,512]{2,1,0:T(8,128)}, u32[]{:S(2)}, u32[]{:S(2)}) async-start(f32[8,32,512]{2,1,0:T(8,128)} %owner_grads.1), calls=%async_computation.3 | async-start | bytes 1048576 | tf_op jit(solution)/shard_map/all_to_all | solution.py:376
